TPU v7x, 128 devices: a whole 4x4x4 slice. The times are simulated.
128 devices in a mesh: gx: 16 (over x, y), gy: 8 (over z, core).
Axes of the slice: x: 4, y: 4, z: 4, core: 2. Of those that a mesh axis runs over, the one named last changes fastest.
Arguments:
- fields: float32 [8, 32, 65536], P(None, None, ('gx', 'gy')), may hold values from -2 to 30, as said below
- refined: int32 [32, 16], replicated, may hold values from 0 to 1, as said below
Outputs:
- advanced: float32 [8, 32, 40960], P(None, None, ('gx', 'gy'))
Inputs may be any that keep to these rules, and one draw needn't show every extreme that they name: Counting one block for a root with refined 0 and four for a root with refined 1, in order of L (gx major) and of the tiles' roots, the blocks before device L number 10 * L plus or minus at most 3; both 10 * L + 3 and 10 * L - 3 occur in every draw, and the blocks number 10 per device in all. `fields`: every slot, live or not, holds a state of density 0.2 to 2, pressure 0.5 to 18, and velocity and field components of size under 0.9.
All inputs are finite; a program needn't handle non-finite values.
Results may differ from a plain program's by a relative error of at most 0.0003.
Values sent between devices are 32-bit elements; how exact they have to be, the bound alone decides.
A program may use at most 64 MiB of HBM per device.

v0:
```python
import functools

import jax
import jax.numpy as jnp
from jax import lax
from jax.experimental import pallas as pl
from jax.experimental.pallas import tpu as pltpu
from jax.sharding import PartitionSpec as P

BS = 32
CAP = 10
EXT = BS + 8
GAMMA = 5.0 / 3.0
COURANT = 0.2
MESH = pl.DeviceIdType.MESH
F32 = jnp.float32

BASE = (4, 140, 276)
PAD_ROWS = 352
ROWS = (0, 8, 16, 24, 32)
FACE1 = (0, 8, 16, 24, 31)
MID = (1, 9, 17, 25, 31)
SLOPE = (2, 10, 18, 26, 29)
FACE2 = (3, 11, 19, 27, 28)
LAST = (4, 12, 20, 28)


def lanes(rows):
    return lax.broadcasted_iota(jnp.int32, (rows, 128), 1)


def roll(x, by):
    if isinstance(by, int):
        by = by % 128
        return x if by == 0 else pltpu.roll(x, by, 1)
    return pltpu.roll(x, lax.rem(by + 256, 128), 1)


def recip(x):
    r = pltpu.reciprocal(x, approx=True)
    return r * (2.0 - x * r)


def root(x):
    return x * lax.rsqrt(jnp.maximum(x, 1e-30))


def limited(value, other):
    return jnp.minimum(jnp.maximum(value, jnp.minimum(other, 0.0)), jnp.maximum(other, 0.0))


def primitive(u):
    rho, mx, my, mz, energy, bx, by, bz = u
    inv = recip(rho)
    vx, vy, vz = mx * inv, my * inv, mz * inv
    half_b2 = 0.5 * (bx * bx + by * by + bz * bz)
    kinetic = 0.5 * (mx * vx + my * vy + mz * vz)
    pressure = (GAMMA - 1.0) * (energy - kinetic - half_b2)
    return inv, vx, vy, vz, pressure, half_b2


def fast_pair(inv, pressure, half_b2, trans_x, trans_y):
    sound = GAMMA * pressure * inv
    alfven = 2.0 * half_b2 * inv
    total = sound + alfven
    diff = sound - alfven
    square = diff * diff
    four = 4.0 * sound * inv
    fast_x = root(0.5 * (total + root(square + four * trans_x)))
    fast_y = root(0.5 * (total + root(square + four * trans_y)))
    return fast_x, fast_y


def cell_state(u):
    rho, mx, my, mz, energy, bx, by, bz = u
    inv, vx, vy, vz, pressure, half_b2 = primitive(u)
    xx, yy, zz = bx * bx, by * by, bz * bz
    fast_x, fast_y = fast_pair(inv, pressure, half_b2, yy + zz, xx + zz)
    total_p = pressure + half_b2
    enthalpy = energy + total_p
    vb = vx * bx + vy * by + vz * bz
    cross = mx * vy - bx * by
    emf = by * vx - bx * vy
    flux_x = (mx * vx + total_p - xx, cross, mx * vz - bx * bz, enthalpy * vx - bx * vb, emf, bz * vx - bx * vz)
    flux_y = (cross, my * vy + total_p - yy, my * vz - by * bz, enthalpy * vy - by * vb, -emf, bz * vy - by * vz)
    return flux_x, (vx - fast_x, vx + fast_x), flux_y, (vy - fast_y, vy + fast_y)


def edge_weights(slow_l, fast_l, slow_r, fast_r):
    slow = jnp.minimum(jnp.minimum(slow_l, slow_r), 0.0)
    fast = jnp.maximum(jnp.maximum(fast_l, fast_r), 0.0)
    inv = recip(fast - slow)
    a = fast * inv
    b = -slow * inv
    return slow, fast, a, b, slow * a


def side(w, normal):
    rho, vx, vy, vz, pressure, bx, by, bz = w
    vn, vt, bn, bt = (vx, vy, bx, by) if normal == 1 else (vy, vx, by, bx)
    inv = recip(rho)
    trans = bt * bt + bz * bz
    nn = bn * bn
    b2 = trans + nn
    sound = GAMMA * pressure * inv
    alfven = b2 * inv
    diff = sound - alfven
    fast = root(0.5 * (sound + alfven + root(diff * diff + 4.0 * sound * inv * trans)))
    half_b2 = 0.5 * b2
    total_p = pressure + half_b2
    energy = 1.5 * pressure + half_b2 + 0.5 * rho * (vn * vn + vt * vt + vz * vz)
    vb = vn * bn + vt * bt + vz * bz
    return vn - fast, vn + fast, (rho, vn, vt, vz, bn, bt, bz, energy, total_p, total_p - nn, vb)


def moved(state, speed):
    rho, vn, vt, vz, bn, bt, bz, energy, total_p, stress, vb = state
    rel = vn - speed
    mass = rho * rel
    return (
        mass,
        mass * vn + stress,
        mass * vt - bn * bt,
        mass * vz - bn * bz,
        energy * rel + total_p * vn - bn * vb,
        bt * rel - bn * vt,
        bz * rel - bn * vz,
    )


def face_flux(left, right, normal):
    slow_l, fast_l, state_l = side(left, normal)
    slow_r, fast_r, state_r = side(right, normal)
    slow, fast, a, b, c = edge_weights(slow_l, fast_l, slow_r, fast_r)
    from_l = moved(state_l, slow)
    from_r = moved(state_r, fast)
    mass, mn, mt, mz, en, bt, bz = (a * p + b * q for p, q in zip(from_l, from_r))
    bn = c * (state_r[4] - state_l[4])
    if normal == 1:
        return (mass, mn, mt, mz, en, bn, bt, bz)
    return (mass, mt, mn, mz, en, bt, bn, bz)


def kernel(ngx, ngy, ref_s, ref_v, fields, out, *scratch):
    (X, F, C, G, U, ML, MR, RL, RR, SR, RB, SK, RK, SY, RY, VM, P1, P2, SX, GX, DY, W, RA, EA, GX2, O, in_sem, send, recv) = scratch
    gx = lax.axis_index("gx")
    gy = lax.axis_index("gy")
    me = gx * ngy + gy
    load = pltpu.make_async_copy(fields, X, in_sem)
    load.start()

    def at(dx, dy):
        return lax.rem(gx + dx + ngx, ngx), lax.rem(gy + dy + ngy, ngy)

    partners = [at(0, s) for s in range(1, ngy)] + [at(s, 0) for s in range(1, ngx)]
    partners += [at(1, 1), at(1, -1), at(-1, 1), at(-1, -1)]
    barrier = pltpu.get_barrier_semaphore()
    for who in partners:
        pl.semaphore_signal(barrier, inc=1, device_id=who, device_id_type=MESH)

    sems = iter(range(64))

    def remote(src, dst, who):
        i = next(sems)
        return pltpu.make_async_remote_copy(
            src_ref=src, dst_ref=dst, send_sem=send.at[i], recv_sem=recv.at[i], device_id=who, device_id_type=MESH
        )

    def flags_of(tile):
        tx, ty = lax.div(tile, ngy), lax.rem(tile, ngy)
        return [ref_s[2 * tx + r // 2, 2 * ty + r % 2] for r in range(4)]

    tile_of = lax.broadcasted_iota(jnp.int32, (2 * ngx, 2 * ngy), 0) // 2 * ngy
    tile_of = tile_of + lax.broadcasted_iota(jnp.int32, (2 * ngx, 2 * ngy), 1) // 2
    before = jnp.sum(jnp.where(tile_of < me, ref_v[...], 0))
    excess = 4 * me + 3 * before - CAP * me
    mine = flags_of(me)
    prev = flags_of(lax.rem(me + ngx * ngy - 1, ngx * ngy))
    following = flags_of(lax.rem(me + 1, ngx * ngy))

    def count_of(fl):
        return 4 + 3 * (fl[0] + fl[1] + fl[2] + fl[3])

    count = count_of(mine)

    def ge(a, b):
        return jnp.where(a >= b, 1, 0)

    def find(index, fl):
        index = jnp.clip(index, 0, count_of(fl) - 1)
        p1 = 1 + 3 * fl[0]
        p2 = p1 + 1 + 3 * fl[1]
        p3 = p2 + 1 + 3 * fl[2]
        a1, a2, a3 = ge(index, p1), ge(index, p2), ge(index, p3)
        child = index - (a1 * p1 + a2 * (p2 - p1) + a3 * (p3 - p2))
        flag = fl[0] + a1 * (fl[1] - fl[0]) + a2 * (fl[2] - fl[1]) + a3 * (fl[3] - fl[2])
        rx = a2
        ry = a1 + a2 + a3 - 2 * rx
        cx, cy = child & 1, child >> 1
        row = flag * (BASE[0] + 136 * ry + 64 * rx + 32 * cx) + (1 - flag) * (BASE[2] + 32 * rx)
        lane = 32 * (flag * cy + (1 - flag) * ry)
        return row, lane, flag

    place = {w: find(w - excess, mine) for w in range(-3, 13)}
    wide = {}
    for w in range(CAP):
        flag = place[w][2]
        index = w - excess
        if w < 3:
            flag = jnp.where(index >= 0, flag, find(index + count_of(prev), prev)[2])
        if w >= 7:
            flag = jnp.where(index < count, flag, find(index - count, following)[2])
        wide[w] = 0.5 + 0.5 * flag.astype(F32)

    lane8, lane32, lane40 = lanes(8), lanes(32), lanes(EXT)
    load.wait()

    def build(c, carry):
        for rx in range(2):
            a = X[c, :, 256 * rx : 256 * rx + 128]
            b = X[c, :, 256 * rx + 128 : 256 * rx + 256]
            a32, a64, b64, b32 = roll(a, -32), roll(a, -64), roll(b, 64), roll(b, 32)
            top = jnp.where(lane32 < 32, a, jnp.where(lane32 < 64, a32, jnp.where(lane32 < 96, b64, b32)))
            low = jnp.where(lane32 < 32, a32, jnp.where(lane32 < 64, a64, jnp.where(lane32 < 96, b32, b)))
            z = jnp.where(lane32 < 32, a, b32)
            z = jnp.take_along_axis(z, lane32 // 2, axis=1)
            F[c, pl.ds(64 * rx, 32, stride=2), :] = z
            F[c, pl.ds(64 * rx + 1, 32, stride=2), :] = z
            keep = jnp.where(lane32 < 64, mine[2 * rx], mine[2 * rx + 1]) > 0
            F[c, 64 * rx : 64 * rx + 32, :] = jnp.where(keep, top, F[c, 64 * rx : 64 * rx + 32, :])
            F[c, 64 * rx + 32 : 64 * rx + 64, :] = jnp.where(keep, low, F[c, 64 * rx + 32 : 64 * rx + 64, :])
        for rx in range(2):
            s = F[c, pl.ds(64 * rx, 32, stride=2), :] + F[c, pl.ds(64 * rx + 1, 32, stride=2), :]
            s = (s + roll(s, -1)) * 0.25
            C[c, 32 * rx : 32 * rx + 32, :] = jnp.take_along_axis(s, lane32 * 2 % 128, axis=1)
        SR[0, c, 0:4, :] = F[c, 124:128, :]
        SR[0, c, 4:8, :] = C[c, 60:64, :]
        SR[1, c, 0:4, :] = F[c, 0:4, :]
        SR[1, c, 4:8, :] = C[c, 0:4, :]
        return carry

    lax.fori_loop(0, 8, build, 0)

    def corners(c, carry):
        s = 8 * c + 4
        inside = (lane8 >= s - 4) & (lane8 < s + 4)
        return tuple(jnp.where(inside, roll(SR[d, c], s), carry[d]) for d in range(2))

    zero8 = jnp.zeros((8, 128), F32)
    down, up = lax.fori_loop(0, 8, corners, (zero8, zero8))
    SK[0] = down
    SK[1] = up

    def columns(h, carry):
        for q in range(4):
            acc_r, acc_l = zero8, zero8
            for cc in range(4):
                for k in range(6):
                    s = 32 * cc + 4 * k + 4
                    source = F if k < 4 else C
                    row = 32 * (k if k < 4 else k - 4) + 8 * q
                    x = roll(source[4 * h + cc, row : row + 8, :], s)
                    acc_r = jnp.where((lane8 >= s - 4) & (lane8 < s), x, acc_r)
                    acc_l = jnp.where((lane8 >= s) & (lane8 < s + 4), x, acc_l)
            SY[0, h, 8 * q : 8 * q + 8, :] = acc_r
            SY[1, h, 8 * q : 8 * q + 8, :] = acc_l
        return carry

    lax.fori_loop(0, 2, columns, 0)

    ghosts = [
        remote(SY.at[0], RY.at[0], at(0, 1)),
        remote(SY.at[1], RY.at[1], at(0, -1)),
        remote(SR.at[0], RB.at[0], at(1, 0)),
        remote(SR.at[1], RB.at[1], at(-1, 0)),
        remote(SK.at[0], RK.at[0], at(1, 1)),
        remote(SK.at[0], RK.at[1], at(1, -1)),
        remote(SK.at[1], RK.at[2], at(-1, 1)),
        remote(SK.at[1], RK.at[3], at(-1, -1)),
    ]
    pl.semaphore_wait(barrier, len(partners))
    for copy in ghosts:
        copy.start()

    peak = zero8
    for r in range(4):
        on = mine[r] > 0
        weight = jnp.where(lane8 < 32, jnp.where(on, 1.0, 0.5), jnp.where(on, 1.0, 0.0)).astype(F32)
        for q in range(4):
            u = [X[c, 8 * q : 8 * q + 8, 128 * r : 128 * r + 128] for c in range(8)]
            inv, vx, vy, vz, pressure, half_b2 = primitive(u)
            xx, yy, zz = (b * b for b in u[5:])
            fast_x, fast_y = fast_pair(inv, pressure, half_b2, yy + zz, xx + zz)
            rate = jnp.maximum(jnp.abs(vx) + fast_x, jnp.abs(vy) + fast_y)
            peak = jnp.maximum(peak, jnp.where(weight > 0.0, rate * weight, 0.0))
    VM[0] = peak
    round1 = [remote(VM.at[0], P1.at[s - 1], at(0, s)) for s in range(1, ngy)]
    for copy in round1:
        copy.start()

    for copy in ghosts:
        copy.wait_recv()

    def fill(h, carry):
        for cc in range(4):
            c = 4 * h + cc
            for d in range(2):
                from_l = roll(RK[2 * d], -8 * c)
                from_r = roll(RK[2 * d + 1], 64 - 8 * c)
                row = RB[d, c]
                row4, row60 = roll(row, 4), roll(row, -60)
                start = [b + (0, 132)[d] for b in BASE[:2]] + [BASE[2] + (0, 68)[d]]
                G[c, start[0] : start[0] + 4, :] = jnp.where(lane8 < 4, from_l, row4)[0:4]
                G[c, start[1] : start[1] + 4, :] = jnp.where(lane8 < 68, row60, from_r)[0:4]
                G[c, start[2] : start[2] + 4, :] = jnp.where(lane8 < 4, from_l, jnp.where(lane8 < 68, row4, from_r))[4:8]
            for k in range(6):
                s = 32 * cc + 4 * k
                from_l = roll(RY[0, h], -s)
                from_r = roll(RY[1, h], 64 - s)
                if k < 4:
                    x = F[c, 32 * k : 32 * k + 32, :]
                    row = BASE[0] + 4 + 32 * k
                    G[c, row : row + 32, :] = jnp.where(lane32 < 4, from_l, roll(x, 4))
                    row = BASE[1] + 4 + 32 * k
                    G[c, row : row + 32, :] = jnp.where(lane32 < 68, roll(x, -60), from_r)
                else:
                    x = C[c, 32 * (k - 4) : 32 * (k - 4) + 32, :]
                    row = BASE[2] + 4 + 32 * (k - 4)
                    G[c, row : row + 32, :] = jnp.where(lane32 < 4, from_l, jnp.where(lane32 < 68, roll(x, 4), from_r))
        return carry

    lax.fori_loop(0, 2, fill, 0)

    def gather(dst, which):
        def body(c, carry):
            parts = [roll(G[c, pl.ds(place[w][0], EXT), :], EXT * g - place[w][1]) for g, w in enumerate(which)]
            x = parts[0]
            for g, part in enumerate(parts[1:]):
                x = jnp.where(lane40 < EXT * (g + 1), x, part)
            dst[c] = x
            return carry

        lax.fori_loop(0, 8, body, 0)

    gather(MR, (10, 11, 12))
    gather(ML, (-3, -2, -1))
    carry_up = lax.div(gy + 1, ngy)
    carry_down = lax.div(ngy - gy, ngy)
    ahead = (lax.rem(gx + carry_up, ngx), lax.rem(gy + 1, ngy))
    behind = (lax.rem(gx + ngx - carry_down, ngx), lax.rem(gy + ngy - 1, ngy))
    moves = [remote(MR, RL, ahead), remote(ML, RR, behind)]
    for copy in moves:
        copy.start()

    for copy in round1:
        copy.wait_recv()
    for s in range(ngy - 1):
        peak = jnp.maximum(peak, P1[s])
    VM[1] = peak
    round2 = [remote(VM.at[1], P2.at[s - 1], at(s, 0)) for s in range(1, ngx)]
    for copy in round2:
        copy.start()

    gather(U.at[0], (3, 4, 5))
    gather(U.at[1], (6,))
    gather(U.at[2], (0, 1, 2))
    gather(U.at[3], (7, 8, 9))

    def first(t, carry):
        for r in ROWS:
            u = [U[t, c, r : r + 8, :] for c in range(8)]
            flux_x, edge_x, flux_y, edge_y = cell_state(u)
            for i, v in enumerate(flux_x + edge_x):
                SX[i, r : r + 8, :] = v
            _, _, a, b, w = edge_weights(*edge_y, roll(edge_y[0], -1), roll(edge_y[1], -1))
            cell = (u[2],) + flux_y[:5] + (None,) + flux_y[5:]
            for c in range(8):
                jump = w * (roll(u[c], -1) - u[c])
                flux = jump if cell[c] is None else a * cell[c] + b * roll(cell[c], -1) + jump
                DY[t, c, r : r + 8, :] = flux - roll(flux, 1)
        for r in FACE1:
            edges = [SX[i, r + d : r + d + 8, :] for d in range(2) for i in (6, 7)]
            _, _, a, b, w = edge_weights(*edges)
            for c in range(8):
                low, high = U[t, c, r : r + 8, :], U[t, c, r + 1 : r + 9, :]
                flux = w * (high - low)
                if c == 0:
                    flux = a * U[t, 1, r : r + 8, :] + b * U[t, 1, r + 1 : r + 9, :] + flux
                elif c != 5:
                    i = c - 1 if c < 5 else c - 2
                    flux = a * SX[i, r : r + 8, :] + b * SX[i, r + 1 : r + 9, :] + flux
                GX[t, c, r : r + 8, :] = flux
        return carry

    lax.fori_loop(0, 2, first, 0)

    for copy in moves:
        copy.wait_recv()

    def merge(c, carry):
        U[2, c] = jnp.where(lane40 // EXT < excess, RL[c], U[2, c])
        U[3, c] = jnp.where(lane40 // EXT + 7 >= count + excess, RR[c], U[3, c])
        return carry

    lax.fori_loop(0, 8, merge, 0)
    lax.fori_loop(2, 4, first, 0)

    for copy in round2:
        copy.wait_recv()
    for s in range(ngx - 1):
        peak = jnp.maximum(peak, P2[s])
    peak = jnp.max(jnp.max(peak, axis=0, keepdims=True), axis=1, keepdims=True)
    time_step = COURANT / jnp.broadcast_to(peak, (8, 128))

    def widths(ws):
        v = jnp.full((8, 128), wide[ws[0]], F32)
        for g, w in enumerate(ws[1:]):
            v = jnp.where(lane8 < EXT * (g + 1), v, wide[w])
        return v

    VM[2] = time_step * widths((3, 4, 5))
    VM[3] = time_step * widths((6,))
    VM[4] = time_step * widths((0, 1, 2))
    VM[5] = time_step * widths((7, 8, 9))

    def second(t, carry):
        rate = VM[2 + t]
        half = 0.5 * rate
        for r in MID:
            u = []
            for c in range(8):
                change = GX[t, c, r : r + 8, :] - GX[t, c, r - 1 : r + 7, :] + DY[t, c, r : r + 8, :]
                u.append(U[t, c, r : r + 8, :] - half * change)
            _, vx, vy, vz, pressure, _ = primitive(u)
            for c, v in enumerate((u[0], vx, vy, vz, pressure, u[5], u[6], u[7])):
                W[c, r : r + 8, :] = v
        for r in SLOPE:
            for c in range(8):
                w = [W[c, r + d : r + d + 8, :] for d in (-1, 0, 1, 2)]
                low, d, high = w[1] - w[0], w[2] - w[1], w[3] - w[2]
                rise = limited(0.5 * d + (low - high) * (1.0 / 12.0), d)
                RA[c, r : r + 8, :] = rise
                EA[c, r : r + 8, :] = d - rise
        for r in FACE2:
            left, right = [], []
            for c in range(8):
                rise, rise_next = RA[c, r : r + 8, :], RA[c, r + 1 : r + 9, :]
                fall, fall_next = EA[c, r - 1 : r + 7, :], EA[c, r : r + 8, :]
                left.append(W[c, r : r + 8, :] + limited(rise, 2.0 * fall))
                right.append(W[c, r + 1 : r + 9, :] - limited(fall_next, 2.0 * rise_next))
            for c, v in enumerate(face_flux(left, right, 1)):
                GX2[c, r : r + 8, :] = v
        for r in LAST:
            left, right = [], []
            for c in range(8):
                w = W[c, r : r + 8, :]
                ahead_w = roll(w, -1)
                d = ahead_w - w
                rise = limited(0.5 * d + (roll(d, 1) - roll(d, -1)) * (1.0 / 12.0), d)
                fall = d - rise
                left.append(w + limited(rise, 2.0 * roll(fall, 1)))
                right.append(ahead_w - limited(fall, 2.0 * roll(rise, -1)))
            for c, v in enumerate(face_flux(left, right, 2)):
                change = GX2[c, r : r + 8, :] - GX2[c, r - 1 : r + 7, :] + (v - roll(v, 1))
                O[t, c, r - 4 : r + 4, :] = U[t, c, r : r + 8, :] - rate * change
        return carry

    lax.fori_loop(0, 4, second, 0)

    def finish(c, carry):
        o = [O[t, c] for t in range(4)]
        o0 = jnp.where(lane32 < 32, roll(o[2], -4), jnp.where(lane32 < 64, roll(o[2], -12), roll(o[2], -20)))
        out[c, :, 0:128] = jnp.where(lane32 < 96, o0, roll(o[0], 92))
        o1 = jnp.where(lane32 < 32, roll(o[0], -44), roll(o[0], -52))
        out[c, :, 128:256] = jnp.where(lane32 < 64, o1, jnp.where(lane32 < 96, roll(o[1], 60), roll(o[3], 92)))
        o2 = jnp.where(lane32 < 32, roll(o[3], -44), roll(o[3], -52))
        out[c, :, 256:320] = o2[:, 0:64]
        return carry

    lax.fori_loop(0, 8, finish, 0)

    for copy in ghosts + moves + round1 + round2:
        copy.wait_send()


def shards(ngx, ngy, fields, refined):
    vmem = lambda *shape: pltpu.VMEM(shape, F32)
    scratch = [
        vmem(8, 32, 512),
        vmem(8, 128, 128),
        vmem(8, 64, 128),
        vmem(8, PAD_ROWS, 128),
        vmem(4, 8, EXT, 128),
        vmem(8, EXT, 128),
        vmem(8, EXT, 128),
        vmem(8, EXT, 128),
        vmem(8, EXT, 128),
        vmem(2, 8, 8, 128),
        vmem(2, 8, 8, 128),
        vmem(2, 8, 128),
        vmem(4, 8, 128),
        vmem(2, 2, 32, 128),
        vmem(2, 2, 32, 128),
        vmem(6, 8, 128),
        vmem(ngy - 1, 8, 128),
        vmem(ngx - 1, 8, 128),
        vmem(8, EXT, 128),
        vmem(4, 8, EXT, 128),
        vmem(4, 8, EXT, 128),
        vmem(8, EXT, 128),
        vmem(8, EXT, 128),
        vmem(8, EXT, 128),
        vmem(8, EXT, 128),
        vmem(4, 8, BS, 128),
        pltpu.SemaphoreType.DMA,
        pltpu.SemaphoreType.DMA((ngx + ngy + 8,)),
        pltpu.SemaphoreType.DMA((ngx + ngy + 8,)),
    ]
    return pl.pallas_call(
        functools.partial(kernel, ngx, ngy),
        out_shape=jax.ShapeDtypeStruct((8, BS, CAP * BS), F32),
        in_specs=[
            pl.BlockSpec(memory_space=pltpu.SMEM),
            pl.BlockSpec(memory_space=pltpu.VMEM),
            pl.BlockSpec(memory_space=pl.ANY),
        ],
        out_specs=pl.BlockSpec(memory_space=pltpu.VMEM),
        scratch_shapes=scratch,
        compiler_params=pltpu.CompilerParams(
            collective_id=0, has_side_effects=True, vmem_limit_bytes=32 * 1024 * 1024
        ),
    )(refined, refined, fields)


def solution(mesh):
    ngx, ngy = mesh.shape["gx"], mesh.shape["gy"]
    return jax.shard_map(
        functools.partial(shards, ngx, ngy),
        mesh=mesh,
        in_specs=(P(None, None, ("gx", "gy")), P()),
        out_specs=P(None, None, ("gx", "gy")),
        check_vma=False,
    )
```

profile of v0, /device:TPU:0, one launch (start us, length us, event | category | flops | bytes accessed | tf_op | source)
XLA Modules:
  0.0 31.6 jit_solution(9608317488896711969)
XLA Ops:
  0.0 0.8 %copy.3.ref_s.ref_v = s32[32,16]{1,0:T(8,128)S(1)} copy(s32[32,16]{0,1:T(8,128)} %param.3) | data formatting | bytes 4096 | tf_op args[1]
  0.8 0.0 copy-start
  0.8 1.0 %copy-done = f32[8,32,512]{2,1,0:T(8,128)S(1)} copy-done((f32[8,32,512]{2,1,0:T(8,128)S(1)}, f32[8,32,512]{2,1,0:T(8,128)}, u32[]{:S(2)}) %copy-start) | copy-done | bytes 524312
  1.8 29.1 %shard_map.28 = f32[8,32,320]{2,1,0:T(8,128)S(1)} custom-call(s32[32,16]{1,0:T(8,128)S(1)} %copy.3.ref_s.ref_v, s32[32,16]{1,0:T(8,128)S(1)} %copy.3.ref_s.ref_v, f32[8,32,512]{2,1,0:T(8,128)S(1)} %copy-done), custom_call_target="tpu_custom_call" | custom-call | tf_op jit(solution)/shard_map/pallas_call | solution.py:519
  30.9 0.7 %copy.6 = f32[8,32,320]{2,1,0:T(8,128)} copy(f32[8,32,320]{2,1,0:T(8,128)S(1)} %shard_map.28) | data formatting | bytes 655360
Async XLA Ops:
  0.8 1.0 %copy-start = (f32[8,32,512]{2,1,0:T(8,128)S(1)}, f32[8,32,512]{2,1,0:T(8,128)}, u32[]{:S(2)}) copy-start(f32[8,32,512]{2,1,0:T(8,128)} %fields.1) | copy-start | bytes 1572868
where the time goes:
time: 31.8 us; the launch traced here: 31.6 us
  Pallas kernels  29.1 us (92%)
  local copies, waits for them, and re-layouts  2.56 us (8%)
    pallas_call x1, Pallas kernels, shards(): pl.pallas_call(functools.partial(kernel, ngx, ngy), out_shape=jax.ShapeDt...  29.1 us
    unnamed x4, local copies, waits for them, and re-layouts  2.56 us

commit v1 on v0

v1 whole, which is shorter than its diff:
```python
import functools

import jax
import jax.numpy as jnp
from jax import lax
from jax.experimental import pallas as pl
from jax.experimental.pallas import tpu as pltpu
from jax.sharding import PartitionSpec as P

BS = 32
CAP = 10
EXT = BS + 8
GAMMA = 5.0 / 3.0
COURANT = 0.2
MESH = pl.DeviceIdType.MESH
F32 = jnp.float32

FINE = (4, 140)
COARSE = (276, 348)
PAD_ROWS = 424
ROWS = (0, 8, 16, 24, 32)
FACE1 = (0, 8, 16, 24, 31)
MID = (1, 9, 17, 25, 31)
SLOPE = (2, 10, 18, 26, 29)
FACE2 = (3, 11, 19, 27, 28)
LAST = (4, 12, 20, 28)


def lanes(rows):
    return lax.broadcasted_iota(jnp.int32, (rows, 128), 1)


def roll(x, by):
    if isinstance(by, int):
        by = by % 128
        return x if by == 0 else pltpu.roll(x, by, 1)
    return pltpu.roll(x, lax.rem(by + 256, 128), 1)


def recip(x):
    r = pltpu.reciprocal(x, approx=True)
    return r * (2.0 - x * r)


def root(x):
    return x * lax.rsqrt(jnp.maximum(x, 1e-30))


def limited(value, other):
    return jnp.minimum(jnp.maximum(value, jnp.minimum(other, 0.0)), jnp.maximum(other, 0.0))


def primitive(u):
    rho, mx, my, mz, energy, bx, by, bz = u
    inv = recip(rho)
    vx, vy, vz = mx * inv, my * inv, mz * inv
    half_b2 = 0.5 * (bx * bx + by * by + bz * bz)
    kinetic = 0.5 * (mx * vx + my * vy + mz * vz)
    pressure = (GAMMA - 1.0) * (energy - kinetic - half_b2)
    return inv, vx, vy, vz, pressure, half_b2


def fast_pair(inv, pressure, half_b2, trans_x, trans_y):
    sound = GAMMA * pressure * inv
    alfven = 2.0 * half_b2 * inv
    total = sound + alfven
    diff = sound - alfven
    square = diff * diff
    four = 4.0 * sound * inv
    fast_x = root(0.5 * (total + root(square + four * trans_x)))
    fast_y = root(0.5 * (total + root(square + four * trans_y)))
    return fast_x, fast_y


def cell_state(u):
    rho, mx, my, mz, energy, bx, by, bz = u
    inv, vx, vy, vz, pressure, half_b2 = primitive(u)
    xx, yy, zz = bx * bx, by * by, bz * bz
    fast_x, fast_y = fast_pair(inv, pressure, half_b2, yy + zz, xx + zz)
    total_p = pressure + half_b2
    enthalpy = energy + total_p
    vb = vx * bx + vy * by + vz * bz
    cross = mx * vy - bx * by
    emf = by * vx - bx * vy
    flux_x = (mx * vx + total_p - xx, cross, mx * vz - bx * bz, enthalpy * vx - bx * vb, emf, bz * vx - bx * vz)
    flux_y = (cross, my * vy + total_p - yy, my * vz - by * bz, enthalpy * vy - by * vb, -emf, bz * vy - by * vz)
    return flux_x, (vx - fast_x, vx + fast_x), flux_y, (vy - fast_y, vy + fast_y)


def edge_weights(slow_l, fast_l, slow_r, fast_r):
    slow = jnp.minimum(jnp.minimum(slow_l, slow_r), 0.0)
    fast = jnp.maximum(jnp.maximum(fast_l, fast_r), 0.0)
    inv = recip(fast - slow)
    a = fast * inv
    b = -slow * inv
    return slow, fast, a, b, slow * a


def side(w, normal):
    rho, vx, vy, vz, pressure, bx, by, bz = w
    vn, vt, bn, bt = (vx, vy, bx, by) if normal == 1 else (vy, vx, by, bx)
    inv = recip(rho)
    trans = bt * bt + bz * bz
    nn = bn * bn
    b2 = trans + nn
    sound = GAMMA * pressure * inv
    alfven = b2 * inv
    diff = sound - alfven
    fast = root(0.5 * (sound + alfven + root(diff * diff + 4.0 * sound * inv * trans)))
    half_b2 = 0.5 * b2
    total_p = pressure + half_b2
    energy = 1.5 * pressure + half_b2 + 0.5 * rho * (vn * vn + vt * vt + vz * vz)
    vb = vn * bn + vt * bt + vz * bz
    return vn - fast, vn + fast, (rho, vn, vt, vz, bn, bt, bz, energy, total_p, total_p - nn, vb)


def moved(state, speed):
    rho, vn, vt, vz, bn, bt, bz, energy, total_p, stress, vb = state
    rel = vn - speed
    mass = rho * rel
    return (
        mass,
        mass * vn + stress,
        mass * vt - bn * bt,
        mass * vz - bn * bz,
        energy * rel + total_p * vn - bn * vb,
        bt * rel - bn * vt,
        bz * rel - bn * vz,
    )


def face_flux(left, right, normal):
    slow_l, fast_l, state_l = side(left, normal)
    slow_r, fast_r, state_r = side(right, normal)
    slow, fast, a, b, c = edge_weights(slow_l, fast_l, slow_r, fast_r)
    from_l = moved(state_l, slow)
    from_r = moved(state_r, fast)
    mass, mn, mt, mz, en, bt, bz = (a * p + b * q for p, q in zip(from_l, from_r))
    bn = c * (state_r[4] - state_l[4])
    if normal == 1:
        return (mass, mn, mt, mz, en, bn, bt, bz)
    return (mass, mt, mn, mz, en, bt, bn, bz)


def kernel(ngx, ngy, refined, fields, out, *scratch):
    (ref_s, ref_v, X, J, G, U, ML, MR, SR, RB, SK, RK, SY, RY, VM, P1, P2, SX, GX, DY, W, RA, EA, GX2, O, in_sem, send, recv) = scratch
    gx = lax.axis_index("gx")
    gy = lax.axis_index("gy")
    me = gx * ngy + gy
    load = pltpu.make_async_copy(fields, X, in_sem.at[0])
    load.start()
    load_s = pltpu.make_async_copy(refined, ref_s, in_sem.at[1])
    load_s.start()
    load_v = pltpu.make_async_copy(refined, ref_v, in_sem.at[2])
    load_v.start()

    def at(dx, dy):
        return lax.rem(gx + dx + ngx, ngx), lax.rem(gy + dy + ngy, ngy)

    partners = [at(0, s) for s in range(1, ngy)] + [at(s, 0) for s in range(1, ngx)]
    partners += [at(1, 1), at(1, -1), at(-1, 1), at(-1, -1)]
    barrier = pltpu.get_barrier_semaphore()
    for who in partners:
        pl.semaphore_signal(barrier, inc=1, device_id=who, device_id_type=MESH)

    sems = iter(range(64))

    def remote(src, dst, who):
        i = next(sems)
        return pltpu.make_async_remote_copy(
            src_ref=src, dst_ref=dst, send_sem=send.at[i], recv_sem=recv.at[i], device_id=who, device_id_type=MESH
        )

    def flags_of(tile):
        tx, ty = lax.div(tile, ngy), lax.rem(tile, ngy)
        return [ref_s[2 * ty + r % 2, 2 * tx + r // 2] for r in range(4)]

    load_s.wait()
    mine = flags_of(me)
    lane8, lane32, lane40 = lanes(8), lanes(32), lanes(EXT)
    load.wait()

    zero8 = jnp.zeros((8, 128), F32)
    peak = zero8
    for r in range(4):
        on = mine[r] > 0
        weight = jnp.where(lane8 < 32, jnp.where(on, 1.0, 0.5), jnp.where(on, 1.0, 0.0)).astype(F32)
        for q in range(4):
            u = [X[c, 8 * q : 8 * q + 8, 128 * r : 128 * r + 128] for c in range(8)]
            inv, vx, vy, vz, pressure, half_b2 = primitive(u)
            xx, yy, zz = (b * b for b in u[5:])
            fast_x, fast_y = fast_pair(inv, pressure, half_b2, yy + zz, xx + zz)
            rate = jnp.maximum(jnp.abs(vx) + fast_x, jnp.abs(vy) + fast_y)
            peak = jnp.maximum(peak, jnp.where(weight > 0.0, rate * weight, 0.0))
    VM[0] = peak
    round1 = [remote(VM.at[0], P1.at[s - 1], at(0, s)) for s in range(1, ngy)]
    pl.semaphore_wait(barrier, len(partners))
    for copy in round1:
        copy.start()

    turn_even = (lane32 - 4) % 128 // 2
    turn_half = (2 * ((lane32 - 4) % 64) + 4) % 128
    columns = (lane32 - 4) % 128
    first32, first64, first96 = columns < 32, columns < 64, columns < 96
    for c in range(8):
        for rx in range(2):
            a = X[c, :, 256 * rx : 256 * rx + 128]
            b = X[c, :, 256 * rx + 128 : 256 * rx + 256]
            a28, b36 = roll(a, -28), roll(b, 36)
            top = jnp.where(first32, roll(a, 4), jnp.where(first64, a28, jnp.where(first96, roll(b, 68), b36)))
            low = jnp.where(first32, a28, jnp.where(first64, roll(a, -60), jnp.where(first96, b36, roll(b, 4))))
            z = jnp.where(lane32 < 32, a, roll(b, 32))
            z = jnp.take_along_axis(z, turn_even, axis=1)
            J[c, rx, pl.ds(0, 32, stride=2), :] = z
            J[c, rx, pl.ds(1, 32, stride=2), :] = z
            keep = jnp.where(first64, mine[2 * rx], mine[2 * rx + 1]) > 0
            top = jnp.where(keep, top, J[c, rx, 0:32, :])
            low = jnp.where(keep, low, J[c, rx, 32:64, :])
            for base in FINE:
                row = base + 4 + 64 * rx
                G[c, row : row + 32, :] = top
                G[c, row + 32 : row + 64, :] = low
    for c in range(8):
        for rx in range(2):
            row = FINE[0] + 4 + 64 * rx
            x = G[c, pl.ds(row, 32, stride=2), :] + G[c, pl.ds(row + 1, 32, stride=2), :]
            x = (x + roll(x, -1)) * 0.25
            x = jnp.take_along_axis(x, turn_half, axis=1)
            for base in COARSE:
                G[c, base + 4 + 32 * rx : base + 36 + 32 * rx, :] = x

    for copy in round1:
        copy.wait_recv()
    for s in range(ngy - 1):
        peak = jnp.maximum(peak, P1[s])
    VM[1] = peak
    round2 = [remote(VM.at[1], P2.at[s - 1], at(s, 0)) for s in range(1, ngx)]
    for copy in round2:
        copy.start()

    for h in range(2):
        for q in range(4):
            acc_r, acc_l = zero8, zero8
            for cc in range(4):
                for k in range(6):
                    s = 32 * cc + 4 * k
                    row = (FINE[0] + 4 + 32 * k if k < 4 else COARSE[0] + 4 + 32 * (k - 4)) + 8 * q
                    x = roll(G[4 * h + cc, row : row + 8, :], s)
                    acc_r = jnp.where((lane8 >= s) & (lane8 < s + 4), x, acc_r)
                    acc_l = jnp.where((lane8 >= s + 4) & (lane8 < s + 8), x, acc_l)
            SY[0, h, 8 * q : 8 * q + 8, :] = acc_r
            SY[1, h, 8 * q : 8 * q + 8, :] = acc_l
    ghosts = [remote(SY.at[0], RY.at[0], at(0, 1)), remote(SY.at[1], RY.at[1], at(0, -1))]
    for copy in ghosts:
        copy.start()
    for d in range(2):
        corner = zero8
        fine, coarse = FINE[0] + 4 + (124, 0)[d], COARSE[0] + 4 + (60, 0)[d]
        for c in range(8):
            SR[d, c, 0:4, :] = G[c, fine : fine + 4, :]
            SR[d, c, 4:8, :] = G[c, coarse : coarse + 4, :]
            corner = jnp.where(lane8 // 8 == c, roll(SR[d, c], 8 * c), corner)
        SK[d] = corner
    edges = [
        remote(SR.at[0], RB.at[0], at(1, 0)),
        remote(SR.at[1], RB.at[1], at(-1, 0)),
        remote(SK.at[0], RK.at[0], at(1, 1)),
        remote(SK.at[0], RK.at[1], at(1, -1)),
        remote(SK.at[1], RK.at[2], at(-1, 1)),
        remote(SK.at[1], RK.at[3], at(-1, -1)),
    ]
    for copy in edges:
        copy.start()
    ghosts += edges

    load_v.wait()
    tile_of = lax.broadcasted_iota(jnp.int32, (2 * ngy, 2 * ngx), 1) // 2 * ngy
    tile_of = tile_of + lax.broadcasted_iota(jnp.int32, (2 * ngy, 2 * ngx), 0) // 2
    before = jnp.sum(jnp.where(tile_of < me, ref_v[...], 0))
    excess = 4 * me + 3 * before - CAP * me
    prev = flags_of(lax.rem(me + ngx * ngy - 1, ngx * ngy))
    following = flags_of(lax.rem(me + 1, ngx * ngy))

    def count_of(fl):
        return 4 + 3 * (fl[0] + fl[1] + fl[2] + fl[3])

    count = count_of(mine)

    def ge(a, b):
        return jnp.where(a >= b, 1, 0)

    def find(index, fl):
        index = jnp.clip(index, 0, count_of(fl) - 1)
        p1 = 1 + 3 * fl[0]
        p2 = p1 + 1 + 3 * fl[1]
        p3 = p2 + 1 + 3 * fl[2]
        a1, a2, a3 = ge(index, p1), ge(index, p2), ge(index, p3)
        child = index - (a1 * p1 + a2 * (p2 - p1) + a3 * (p3 - p2))
        flag = fl[0] + a1 * (fl[1] - fl[0]) + a2 * (fl[2] - fl[1]) + a3 * (fl[3] - fl[2])
        rx = a2
        ry = a1 + a2 + a3 - 2 * rx
        cx, cy = child & 1, child >> 1
        row = flag * (FINE[0] + 136 * ry + 64 * rx + 32 * cx) + (1 - flag) * (COARSE[0] + 72 * ry + 32 * rx)
        lane = flag * (64 * ry + 32 * cy) + (1 - flag) * 96 * ry
        return row, lane, flag

    place = {w: find(w - excess, mine) for w in range(-3, 13)}
    wide = {}
    for w in range(CAP):
        flag = place[w][2]
        index = w - excess
        if w < 3:
            flag = jnp.where(index >= 0, flag, find(index + count_of(prev), prev)[2])
        if w >= 7:
            flag = jnp.where(index < count, flag, find(index - count, following)[2])
        wide[w] = 0.5 + 0.5 * flag.astype(F32)

    for copy in ghosts:
        copy.wait_recv()
    left8, right8 = lane8 < 4, (lane8 >= 4) & (lane8 < 8)
    left32, right32 = lane32 < 4, (lane32 >= 4) & (lane32 < 8)
    for d in range(2):
        corner = jnp.where(lane8 % 8 < 4, RK[2 * d], RK[2 * d + 1])
        for c in range(8):
            piece = roll(corner, -8 * c)
            row = RB[d, c]
            for i, mask in enumerate((left8, right8)):
                x = jnp.where(mask, piece, row)
                fine, coarse = FINE[i] + 132 * d, COARSE[i] + 68 * d
                G[c, fine : fine + 4, :] = x[0:4]
                G[c, coarse : coarse + 4, :] = x[4:8]
    for h in range(2):
        low4 = lane32 % 8 < 4
        pair = (jnp.where(low4, RY[0, h], RY[1, h]), jnp.where(low4, RY[1, h], RY[0, h]))
        for cc in range(4):
            for k in range(6):
                x = roll(pair[k % 2], -(32 * cc + 4 * k))
                for i, mask in enumerate((left32, right32)):
                    row = FINE[i] + 4 + 32 * k if k < 4 else COARSE[i] + 4 + 32 * (k - 4)
                    pltpu.store(G.at[4 * h + cc, pl.ds(row, 32), :], x, mask=mask)

    def gather(dst, which):
        for c in range(8):
            parts = [roll(G[c, pl.ds(place[w][0], EXT), :], EXT * g - place[w][1]) for g, w in enumerate(which)]
            x = parts[0]
            for g, part in enumerate(parts[1:]):
                x = jnp.where(lane40 < EXT * (g + 1), x, part)
            dst[c] = x

    gather(MR, (10, 11, 12))
    gather(ML, (-3, -2, -1))
    carry_up = lax.div(gy + 1, ngy)
    carry_down = lax.div(ngy - gy, ngy)
    ahead = (lax.rem(gx + carry_up, ngx), lax.rem(gy + 1, ngy))
    behind = (lax.rem(gx + ngx - carry_down, ngx), lax.rem(gy + ngy - 1, ngy))
    moves = [remote(MR, U.at[4], ahead), remote(ML, U.at[5], behind)]
    for copy in moves:
        copy.start()

    gather(U.at[0], (3, 4, 5))
    gather(U.at[1], (6,))
    gather(U.at[2], (0, 1, 2))
    gather(U.at[3], (7, 8, 9))

    def first(t, carry, pick=lambda t: t):
        at_u = pick(t)
        for r in ROWS:
            u = [U[at_u, c, r : r + 8, :] for c in range(8)]
            flux_x, edge_x, flux_y, edge_y = cell_state(u)
            for i, v in enumerate(flux_x + edge_x):
                SX[i, r : r + 8, :] = v
            _, _, a, b, w = edge_weights(*edge_y, roll(edge_y[0], -1), roll(edge_y[1], -1))
            cell = (u[2],) + flux_y[:5] + (None,) + flux_y[5:]
            for c in range(8):
                jump = w * (roll(u[c], -1) - u[c])
                flux = jump if cell[c] is None else a * cell[c] + b * roll(cell[c], -1) + jump
                DY[t, c, r : r + 8, :] = flux - roll(flux, 1)
        for r in FACE1:
            edges = [SX[i, r + d : r + d + 8, :] for d in range(2) for i in (6, 7)]
            _, _, a, b, w = edge_weights(*edges)
            for c in range(8):
                low, high = U[at_u, c, r : r + 8, :], U[at_u, c, r + 1 : r + 9, :]
                flux = w * (high - low)
                if c == 0:
                    flux = a * U[at_u, 1, r : r + 8, :] + b * U[at_u, 1, r + 1 : r + 9, :] + flux
                elif c != 5:
                    i = c - 1 if c < 5 else c - 2
                    flux = a * SX[i, r : r + 8, :] + b * SX[i, r + 1 : r + 9, :] + flux
                GX[t, c, r : r + 8, :] = flux
        return carry

    lax.fori_loop(0, 2, first, 0)

    for copy in moves:
        copy.wait_recv()

    def pick(t):
        from_left = jnp.where(excess > 0, 4, 2)
        from_right = jnp.where(excess + count < CAP, 5, 3)
        return jnp.where(t == 2, from_left, jnp.where(t == 3, from_right, t))

    lax.fori_loop(2, 4, functools.partial(first, pick=pick), 0)

    for copy in round2:
        copy.wait_recv()
    for s in range(ngx - 1):
        peak = jnp.maximum(peak, P2[s])
    peak = jnp.max(jnp.max(peak, axis=0, keepdims=True), axis=1, keepdims=True)
    time_step = COURANT / jnp.broadcast_to(peak, (8, 128))

    def widths(ws):
        v = jnp.full((8, 128), wide[ws[0]], F32)
        for g, w in enumerate(ws[1:]):
            v = jnp.where(lane8 < EXT * (g + 1), v, wide[w])
        return v

    VM[2] = time_step * widths((3, 4, 5))
    VM[3] = time_step * widths((6,))
    VM[4] = time_step * widths((0, 1, 2))
    VM[5] = time_step * widths((7, 8, 9))

    def second(t, carry):
        rate = VM[2 + t]
        at_u = pick(t)
        half = 0.5 * rate
        for r in MID:
            u = []
            for c in range(8):
                change = GX[t, c, r : r + 8, :] - GX[t, c, r - 1 : r + 7, :] + DY[t, c, r : r + 8, :]
                u.append(U[at_u, c, r : r + 8, :] - half * change)
            _, vx, vy, vz, pressure, _ = primitive(u)
            for c, v in enumerate((u[0], vx, vy, vz, pressure, u[5], u[6], u[7])):
                W[c, r : r + 8, :] = v
        for r in SLOPE:
            for c in range(8):
                w = [W[c, r + d : r + d + 8, :] for d in (-1, 0, 1, 2)]
                low, d, high = w[1] - w[0], w[2] - w[1], w[3] - w[2]
                rise = limited(0.5 * d + (low - high) * (1.0 / 12.0), d)
                RA[c, r : r + 8, :] = rise
                EA[c, r : r + 8, :] = d - rise
        for r in FACE2:
            left, right = [], []
            for c in range(8):
                rise, rise_next = RA[c, r : r + 8, :], RA[c, r + 1 : r + 9, :]
                fall, fall_next = EA[c, r - 1 : r + 7, :], EA[c, r : r + 8, :]
                left.append(W[c, r : r + 8, :] + limited(rise, 2.0 * fall))
                right.append(W[c, r + 1 : r + 9, :] - limited(fall_next, 2.0 * rise_next))
            for c, v in enumerate(face_flux(left, right, 1)):
                GX2[c, r : r + 8, :] = v
        for r in LAST:
            left, right = [], []
            for c in range(8):
                w = W[c, r : r + 8, :]
                ahead_w = roll(w, -1)
                d = ahead_w - w
                rise = limited(0.5 * d + (roll(d, 1) - roll(d, -1)) * (1.0 / 12.0), d)
                fall = d - rise
                left.append(w + limited(rise, 2.0 * roll(fall, 1)))
                right.append(ahead_w - limited(fall, 2.0 * roll(rise, -1)))
            for c, v in enumerate(face_flux(left, right, 2)):
                change = GX2[c, r : r + 8, :] - GX2[c, r - 1 : r + 7, :] + (v - roll(v, 1))
                O[t, c, r - 4 : r + 4, :] = U[at_u, c, r : r + 8, :] - rate * change
        return carry

    lax.fori_loop(0, 4, second, 0)

    for c in range(8):
        o = [O[t, c] for t in range(4)]
        o0 = jnp.where(lane32 < 32, roll(o[2], -4), jnp.where(lane32 < 64, roll(o[2], -12), roll(o[2], -20)))
        out[c, :, 0:128] = jnp.where(lane32 < 96, o0, roll(o[0], 92))
        o1 = jnp.where(lane32 < 32, roll(o[0], -44), roll(o[0], -52))
        out[c, :, 128:256] = jnp.where(lane32 < 64, o1, jnp.where(lane32 < 96, roll(o[1], 60), roll(o[3], 92)))
        o2 = jnp.where(lane32 < 32, roll(o[3], -44), roll(o[3], -52))
        out[c, :, 256:320] = o2[:, 0:64]

    for copy in ghosts + moves + round1 + round2:
        copy.wait_send()


def shards(ngx, ngy, fields, refined):
    vmem = lambda *shape: pltpu.VMEM(shape, F32)
    scratch = [
        pltpu.SMEM((2 * ngy, 2 * ngx), jnp.int32),
        pltpu.VMEM((2 * ngy, 2 * ngx), jnp.int32),
        vmem(8, 32, 512),
        vmem(8, 2, 64, 128),
        vmem(8, PAD_ROWS, 128),
        vmem(6, 8, EXT, 128),
        vmem(8, EXT, 128),
        vmem(8, EXT, 128),
        vmem(2, 8, 8, 128),
        vmem(2, 8, 8, 128),
        vmem(2, 8, 128),
        vmem(4, 8, 128),
        vmem(2, 2, 32, 128),
        vmem(2, 2, 32, 128),
        vmem(6, 8, 128),
        vmem(ngy - 1, 8, 128),
        vmem(ngx - 1, 8, 128),
        vmem(8, EXT, 128),
        vmem(4, 8, EXT, 128),
        vmem(4, 8, EXT, 128),
        vmem(8, EXT, 128),
        vmem(8, EXT, 128),
        vmem(8, EXT, 128),
        vmem(8, EXT, 128),
        vmem(4, 8, BS, 128),
        pltpu.SemaphoreType.DMA((3,)),
        pltpu.SemaphoreType.DMA((ngx + ngy + 8,)),
        pltpu.SemaphoreType.DMA((ngx + ngy + 8,)),
    ]
    return pl.pallas_call(
        functools.partial(kernel, ngx, ngy),
        out_shape=jax.ShapeDtypeStruct((8, BS, CAP * BS), F32),
        in_specs=[
            pl.BlockSpec(memory_space=pltpu.HBM),
            pl.BlockSpec(memory_space=pltpu.HBM),
        ],
        out_specs=pl.BlockSpec(memory_space=pltpu.VMEM),
        scratch_shapes=scratch,
        compiler_params=pltpu.CompilerParams(
            collective_id=0, has_side_effects=True, vmem_limit_bytes=60 * 1024 * 1024
        ),
    )(refined.T, fields)


def solution(mesh):
    ngx, ngy = mesh.shape["gx"], mesh.shape["gy"]
    return jax.shard_map(
        functools.partial(shards, ngx, ngy),
        mesh=mesh,
        in_specs=(P(None, None, ("gx", "gy")), P()),
        out_specs=P(None, None, ("gx", "gy")),
        check_vma=False,
    )
```

time: 31.8 us -> 32.1 us (level)
  Pallas kernels: 29.1 us -> 30.2 us
  local copies, waits for them, and re-layouts: 2.56 us -> 1.77 us
    pallas_call x1, Pallas kernels: 29.1 us -> 30.2 us  [shards(): pl.pallas_call(functools.partial(kernel, ngx, ngy), out_shape=jax.ShapeDt...]
    unnamed x4 -> x1, local copies, waits for them, and re-layouts: 2.56 us -> 1.77 us
where the time goes in v1:
time: 32.1 us; the launch traced here: 31.9 us
  Pallas kernels  30.2 us (94%)
  local copies, waits for them, and re-layouts  1.77 us (6%)
    pallas_call x1, Pallas kernels, shards(): pl.pallas_call(functools.partial(kernel, ngx, ngy), out_shape=jax.ShapeDt...  30.2 us
    unnamed x1, local copies, waits for them, and re-layouts  1.77 us

profile of v1, /device:TPU:0, one launch (start us, length us, event | category | flops | bytes accessed | tf_op | source)
XLA Modules:
  0.0 31.9 jit_solution(6092714268452564323)
XLA Ops:
  0.0 30.2 %shard_map.28 = f32[8,32,320]{2,1,0:T(8,128)} custom-call(s32[16,32]{1,0:T(8,128)} %bitcast.1, f32[8,32,512]{2,1,0:T(8,128)} %fields.1), custom_call_target="tpu_custom_call" | custom-call | tf_op jit(solution)/shard_map/pallas_call | solution.py:512
  30.2 1.8 %copy.4 = f32[8,32,320]{2,1,0:T(8,128)} copy(f32[8,32,320]{2,1,0:T(8,128)} %shard_map.28) | data formatting | bytes 655360

commit v2 on v1

--- a/solution.py
+++ b/solution.py
@@ -143,7 +143,7 @@
 
 
 def kernel(ngx, ngy, refined, fields, out, *scratch):
-    (ref_s, ref_v, X, J, G, U, ML, MR, SR, RB, SK, RK, SY, RY, VM, P1, P2, SX, GX, DY, W, RA, EA, GX2, O, in_sem, send, recv) = scratch
+    (ref_s, ref_v, X, Z, G, U, ML, MR, SR, RB, SK, RK, SY, RY, VM, P1, P2, SX, GX, DY, W, RA, EA, GX2, O, in_sem, send, recv) = scratch
     gx = lax.axis_index("gx")
     gy = lax.axis_index("gy")
     me = gx * ngy + gy
@@ -198,69 +198,83 @@
     for copy in round1:
         copy.start()
 
-    turn_even = (lane32 - 4) % 128 // 2
-    turn_half = (2 * ((lane32 - 4) % 64) + 4) % 128
-    columns = (lane32 - 4) % 128
-    first32, first64, first96 = columns < 32, columns < 64, columns < 96
-    for c in range(8):
-        for rx in range(2):
-            a = X[c, :, 256 * rx : 256 * rx + 128]
-            b = X[c, :, 256 * rx + 128 : 256 * rx + 256]
-            a28, b36 = roll(a, -28), roll(b, 36)
-            top = jnp.where(first32, roll(a, 4), jnp.where(first64, a28, jnp.where(first96, roll(b, 68), b36)))
-            low = jnp.where(first32, a28, jnp.where(first64, roll(a, -60), jnp.where(first96, b36, roll(b, 4))))
-            z = jnp.where(lane32 < 32, a, roll(b, 32))
-            z = jnp.take_along_axis(z, turn_even, axis=1)
-            J[c, rx, pl.ds(0, 32, stride=2), :] = z
-            J[c, rx, pl.ds(1, 32, stride=2), :] = z
-            keep = jnp.where(first64, mine[2 * rx], mine[2 * rx + 1]) > 0
-            top = jnp.where(keep, top, J[c, rx, 0:32, :])
-            low = jnp.where(keep, low, J[c, rx, 32:64, :])
-            for base in FINE:
-                row = base + 4 + 64 * rx
-                G[c, row : row + 32, :] = top
-                G[c, row + 32 : row + 64, :] = low
-    for c in range(8):
-        for rx in range(2):
-            row = FINE[0] + 4 + 64 * rx
-            x = G[c, pl.ds(row, 32, stride=2), :] + G[c, pl.ds(row + 1, 32, stride=2), :]
-            x = (x + roll(x, -1)) * 0.25
-            x = jnp.take_along_axis(x, turn_half, axis=1)
-            for base in COARSE:
-                G[c, base + 4 + 32 * rx : base + 36 + 32 * rx, :] = x
-
-    for copy in round1:
-        copy.wait_recv()
-    for s in range(ngy - 1):
-        peak = jnp.maximum(peak, P1[s])
-    VM[1] = peak
-    round2 = [remote(VM.at[1], P2.at[s - 1], at(s, 0)) for s in range(1, ngx)]
-    for copy in round2:
-        copy.start()
-
-    for h in range(2):
-        for q in range(4):
-            acc_r, acc_l = zero8, zero8
-            for cc in range(4):
-                for k in range(6):
-                    s = 32 * cc + 4 * k
-                    row = (FINE[0] + 4 + 32 * k if k < 4 else COARSE[0] + 4 + 32 * (k - 4)) + 8 * q
-                    x = roll(G[4 * h + cc, row : row + 8, :], s)
-                    acc_r = jnp.where((lane8 >= s) & (lane8 < s + 4), x, acc_r)
-                    acc_l = jnp.where((lane8 >= s + 4) & (lane8 < s + 8), x, acc_l)
-            SY[0, h, 8 * q : 8 * q + 8, :] = acc_r
-            SY[1, h, 8 * q : 8 * q + 8, :] = acc_l
+    def rotate(h, carry):
+        for cc in range(4):
+            c = 4 * h + cc
+            for rx in range(2):
+                for q in range(4):
+                    a = X[c, 8 * q : 8 * q + 8, 256 * rx : 256 * rx + 128]
+                    b = X[c, 8 * q : 8 * q + 8, 256 * rx + 128 : 256 * rx + 256]
+                    a32, b32 = roll(a, -32), roll(b, 32)
+                    top = jnp.where(lane8 < 32, a, jnp.where(lane8 < 64, a32, jnp.where(lane8 < 96, roll(b, 64), b32)))
+                    low = jnp.where(lane8 < 32, a32, jnp.where(lane8 < 64, roll(a, -64), jnp.where(lane8 < 96, b32, b)))
+                    row = FINE[0] + 4 + 64 * rx + 8 * q
+                    G[c, row : row + 8, :] = top
+                    G[c, row + 32 : row + 40, :] = low
+                    Z[c, rx, 8 * q : 8 * q + 8, :] = jnp.where(lane8 < 32, a, b32)
+        return carry
+
+    def spread(h, carry):
+        row8 = lax.broadcasted_iota(jnp.int32, (8, 128), 0)
+        half = row8 % 4 * 2
+        halves = lane8 * 2 % 128
+        for cc in range(4):
+            c = 4 * h + cc
+            for rx in range(2):
+                keep = jnp.where(lane8 < 64, mine[2 * rx], mine[2 * rx + 1]) > 0
+                fine = []
+                for q in range(4):
+                    z = jnp.take_along_axis(Z[c, rx, 8 * q : 8 * q + 8, :], lane8 // 2, axis=1)
+                    for i in range(2):
+                        row = FINE[0] + 4 + 64 * rx + 16 * q + 8 * i
+                        x = jnp.take_along_axis(z, row8 // 2 + 4 * i, axis=0)
+                        x = jnp.where(keep, G[c, row : row + 8, :], x)
+                        G[c, row : row + 8, :] = x
+                        G[c, row + 136 : row + 144, :] = x
+                        x = x + pltpu.roll(x, 7, 0)
+                        fine.append(jnp.take_along_axis(x, half, axis=0))
+                for q in range(4):
+                    x = jnp.where(row8 < 4, fine[2 * q], fine[2 * q + 1])
+                    x = 0.25 * (jnp.take_along_axis(x, halves, axis=1) + jnp.take_along_axis(x, halves + 1, axis=1))
+                    for base in COARSE:
+                        row = base + 4 + 32 * rx + 8 * q
+                        G[c, row : row + 8, :] = x
+        return carry
+
+    lax.fori_loop(0, 2, rotate, 0)
+    lax.fori_loop(0, 2, spread, 0)
+
+    def pack_columns():
+        for h in range(2):
+            for q in range(4):
+                acc_r, acc_l = zero8, zero8
+                for cc in range(4):
+                    for k in range(6):
+                        s = 32 * cc + 4 * k
+                        row = (FINE[0] + 4 + 32 * k if k < 4 else COARSE[0] + 4 + 32 * (k - 4)) + 8 * q
+                        x = roll(G[4 * h + cc, row : row + 8, :], s + 4)
+                        acc_r = jnp.where((lane8 >= s) & (lane8 < s + 4), x, acc_r)
+                        acc_l = jnp.where((lane8 >= s + 4) & (lane8 < s + 8), x, acc_l)
+                SY[0, h, 8 * q : 8 * q + 8, :] = acc_r
+                SY[1, h, 8 * q : 8 * q + 8, :] = acc_l
+
+    pack_columns()
+
     ghosts = [remote(SY.at[0], RY.at[0], at(0, 1)), remote(SY.at[1], RY.at[1], at(0, -1))]
     for copy in ghosts:
         copy.start()
-    for d in range(2):
-        corner = zero8
-        fine, coarse = FINE[0] + 4 + (124, 0)[d], COARSE[0] + 4 + (60, 0)[d]
-        for c in range(8):
-            SR[d, c, 0:4, :] = G[c, fine : fine + 4, :]
-            SR[d, c, 4:8, :] = G[c, coarse : coarse + 4, :]
-            corner = jnp.where(lane8 // 8 == c, roll(SR[d, c], 8 * c), corner)
-        SK[d] = corner
+    def pack_rows():
+        for d in range(2):
+            corner = zero8
+            fine, coarse = FINE[0] + 4 + (124, 0)[d], COARSE[0] + 4 + (60, 0)[d]
+            for c in range(8):
+                SR[d, c, 0:4, :] = G[c, fine : fine + 4, :]
+                SR[d, c, 4:8, :] = G[c, coarse : coarse + 4, :]
+                corner = jnp.where(lane8 // 8 == c, roll(SR[d, c], 8 * c + 4), corner)
+            SK[d] = corner
+
+    pack_rows()
+
     edges = [
         remote(SR.at[0], RB.at[0], at(1, 0)),
         remote(SR.at[1], RB.at[1], at(-1, 0)),
@@ -272,6 +286,15 @@
     for copy in edges:
         copy.start()
     ghosts += edges
+
+    for copy in round1:
+        copy.wait_recv()
+    for s in range(ngy - 1):
+        peak = jnp.maximum(peak, P1[s])
+    VM[1] = peak
+    round2 = [remote(VM.at[1], P2.at[s - 1], at(s, 0)) for s in range(1, ngx)]
+    for copy in round2:
+        copy.start()
 
     load_v.wait()
     tile_of = lax.broadcasted_iota(jnp.int32, (2 * ngy, 2 * ngx), 1) // 2 * ngy
@@ -301,7 +324,7 @@
         ry = a1 + a2 + a3 - 2 * rx
         cx, cy = child & 1, child >> 1
         row = flag * (FINE[0] + 136 * ry + 64 * rx + 32 * cx) + (1 - flag) * (COARSE[0] + 72 * ry + 32 * rx)
-        lane = flag * (64 * ry + 32 * cy) + (1 - flag) * 96 * ry
+        lane = flag * (64 * ry + 32 * cy) + (1 - flag) * 96 * ry - 4
         return row, lane, flag
 
     place = {w: find(w - excess, mine) for w in range(-3, 13)}
@@ -317,27 +340,30 @@
 
     for copy in ghosts:
         copy.wait_recv()
-    left8, right8 = lane8 < 4, (lane8 >= 4) & (lane8 < 8)
-    left32, right32 = lane32 < 4, (lane32 >= 4) & (lane32 < 8)
-    for d in range(2):
-        corner = jnp.where(lane8 % 8 < 4, RK[2 * d], RK[2 * d + 1])
-        for c in range(8):
-            piece = roll(corner, -8 * c)
-            row = RB[d, c]
-            for i, mask in enumerate((left8, right8)):
-                x = jnp.where(mask, piece, row)
-                fine, coarse = FINE[i] + 132 * d, COARSE[i] + 68 * d
-                G[c, fine : fine + 4, :] = x[0:4]
-                G[c, coarse : coarse + 4, :] = x[4:8]
-    for h in range(2):
-        low4 = lane32 % 8 < 4
-        pair = (jnp.where(low4, RY[0, h], RY[1, h]), jnp.where(low4, RY[1, h], RY[0, h]))
-        for cc in range(4):
-            for k in range(6):
-                x = roll(pair[k % 2], -(32 * cc + 4 * k))
-                for i, mask in enumerate((left32, right32)):
-                    row = FINE[i] + 4 + 32 * k if k < 4 else COARSE[i] + 4 + 32 * (k - 4)
-                    pltpu.store(G.at[4 * h + cc, pl.ds(row, 32), :], x, mask=mask)
+    def fill():
+        left8, right8 = lane8 >= 124, lane8 < 4
+        left32, right32 = lane32 >= 124, lane32 < 4
+        for d in range(2):
+            corner = jnp.where(lane8 % 8 < 4, RK[2 * d], RK[2 * d + 1])
+            for c in range(8):
+                piece = roll(corner, -8 * c - 4)
+                row = RB[d, c]
+                for i, mask in enumerate((left8, right8)):
+                    x = jnp.where(mask, piece, row)
+                    fine, coarse = FINE[i] + 132 * d, COARSE[i] + 68 * d
+                    G[c, fine : fine + 4, :] = x[0:4]
+                    G[c, coarse : coarse + 4, :] = x[4:8]
+        for h in range(2):
+            low4 = lane32 % 8 < 4
+            pair = (jnp.where(low4, RY[0, h], RY[1, h]), jnp.where(low4, RY[1, h], RY[0, h]))
+            for cc in range(4):
+                for k in range(6):
+                    x = roll(pair[k % 2], -(32 * cc + 4 * k) - 4)
+                    for i, mask in enumerate((left32, right32)):
+                        row = FINE[i] + 4 + 32 * k if k < 4 else COARSE[i] + 4 + 32 * (k - 4)
+                        pltpu.store(G.at[4 * h + cc, pl.ds(row, 32), :], x, mask=mask)
+
+    fill()
 
     def gather(dst, which):
         for c in range(8):
@@ -391,16 +417,6 @@
 
     lax.fori_loop(0, 2, first, 0)
 
-    for copy in moves:
-        copy.wait_recv()
-
-    def pick(t):
-        from_left = jnp.where(excess > 0, 4, 2)
-        from_right = jnp.where(excess + count < CAP, 5, 3)
-        return jnp.where(t == 2, from_left, jnp.where(t == 3, from_right, t))
-
-    lax.fori_loop(2, 4, functools.partial(first, pick=pick), 0)
-
     for copy in round2:
         copy.wait_recv()
     for s in range(ngx - 1):
@@ -419,7 +435,7 @@
     VM[4] = time_step * widths((0, 1, 2))
     VM[5] = time_step * widths((7, 8, 9))
 
-    def second(t, carry):
+    def second(t, carry, pick=lambda t: t):
         rate = VM[2 + t]
         at_u = pick(t)
         half = 0.5 * rate
@@ -462,16 +478,30 @@
                 O[t, c, r - 4 : r + 4, :] = U[at_u, c, r : r + 8, :] - rate * change
         return carry
 
-    lax.fori_loop(0, 4, second, 0)
-
-    for c in range(8):
-        o = [O[t, c] for t in range(4)]
-        o0 = jnp.where(lane32 < 32, roll(o[2], -4), jnp.where(lane32 < 64, roll(o[2], -12), roll(o[2], -20)))
-        out[c, :, 0:128] = jnp.where(lane32 < 96, o0, roll(o[0], 92))
-        o1 = jnp.where(lane32 < 32, roll(o[0], -44), roll(o[0], -52))
-        out[c, :, 128:256] = jnp.where(lane32 < 64, o1, jnp.where(lane32 < 96, roll(o[1], 60), roll(o[3], 92)))
-        o2 = jnp.where(lane32 < 32, roll(o[3], -44), roll(o[3], -52))
-        out[c, :, 256:320] = o2[:, 0:64]
+    lax.fori_loop(0, 2, second, 0)
+
+    for copy in moves:
+        copy.wait_recv()
+
+    def pick(t):
+        from_left = jnp.where(excess > 0, 4, 2)
+        from_right = jnp.where(excess + count < CAP, 5, 3)
+        return jnp.where(t == 2, from_left, jnp.where(t == 3, from_right, t))
+
+    lax.fori_loop(2, 4, functools.partial(first, pick=pick), 0)
+    lax.fori_loop(2, 4, functools.partial(second, pick=pick), 0)
+
+    def finish():
+        for c in range(8):
+            o = [O[t, c] for t in range(4)]
+            o0 = jnp.where(lane32 < 32, roll(o[2], -4), jnp.where(lane32 < 64, roll(o[2], -12), roll(o[2], -20)))
+            out[c, :, 0:128] = jnp.where(lane32 < 96, o0, roll(o[0], 92))
+            o1 = jnp.where(lane32 < 32, roll(o[0], -44), roll(o[0], -52))
+            out[c, :, 128:256] = jnp.where(lane32 < 64, o1, jnp.where(lane32 < 96, roll(o[1], 60), roll(o[3], 92)))
+            o2 = jnp.where(lane32 < 32, roll(o[3], -44), roll(o[3], -52))
+            out[c, :, 256:320] = o2[:, 0:64]
+
+    finish()
 
     for copy in ghosts + moves + round1 + round2:
         copy.wait_send()
@@ -483,7 +513,7 @@
         pltpu.SMEM((2 * ngy, 2 * ngx), jnp.int32),
         pltpu.VMEM((2 * ngy, 2 * ngx), jnp.int32),
         vmem(8, 32, 512),
-        vmem(8, 2, 64, 128),
+        vmem(8, 2, BS, 128),
         vmem(8, PAD_ROWS, 128),
         vmem(6, 8, EXT, 128),
         vmem(8, EXT, 128),

time: 32.1 us -> 28.3 us (0.88)
  Pallas kernels: 30.2 us -> 26.4 us
    pallas_call x1, Pallas kernels: 30.2 us -> 26.4 us  [shards(): pl.pallas_call(functools.partial(kernel, ngx, ngy), out_shape=jax.ShapeDt...]
where the time goes in v2:
time: 28.3 us; the launch traced here: 28.1 us
  Pallas kernels  26.4 us (93%)
  local copies, waits for them, and re-layouts  1.77 us (6%)
    pallas_call x1, Pallas kernels, shards(): pl.pallas_call(functools.partial(kernel, ngx, ngy), out_shape=jax.ShapeDt...  26.4 us
    unnamed x1, local copies, waits for them, and re-layouts  1.77 us

profile of v2, /device:TPU:0, one launch (start us, length us, event | category | flops | bytes accessed | tf_op | source)
XLA Modules:
  0.0 28.1 jit_solution(11153120173429869089)
XLA Ops:
  0.0 26.4 %shard_map.28 = f32[8,32,320]{2,1,0:T(8,128)} custom-call(s32[16,32]{1,0:T(8,128)} %bitcast.1, f32[8,32,512]{2,1,0:T(8,128)} %fields.1), custom_call_target="tpu_custom_call" | custom-call | tf_op jit(solution)/shard_map/pallas_call | solution.py:542
  26.4 1.8 %copy.4 = f32[8,32,320]{2,1,0:T(8,128)} copy(f32[8,32,320]{2,1,0:T(8,128)} %shard_map.28) | data formatting | bytes 655360

commit v3 on v2

--- a/solution.py
+++ b/solution.py
@@ -142,18 +142,11 @@
     return (mass, mt, mn, mz, en, bt, bn, bz)
 
 
-def kernel(ngx, ngy, refined, fields, out, *scratch):
-    (ref_s, ref_v, X, Z, G, U, ML, MR, SR, RB, SK, RK, SY, RY, VM, P1, P2, SX, GX, DY, W, RA, EA, GX2, O, in_sem, send, recv) = scratch
+def kernel(ngx, ngy, ref_s, ref_v, X, out, *scratch):
+    (Z, G, U, ML, MR, SR, RB, SK, RK, SY, RY, VM, P1, P2, SX, GX, DY, W, RA, EA, GX2, O, send, recv) = scratch
     gx = lax.axis_index("gx")
     gy = lax.axis_index("gy")
     me = gx * ngy + gy
-    load = pltpu.make_async_copy(fields, X, in_sem.at[0])
-    load.start()
-    load_s = pltpu.make_async_copy(refined, ref_s, in_sem.at[1])
-    load_s.start()
-    load_v = pltpu.make_async_copy(refined, ref_v, in_sem.at[2])
-    load_v.start()
-
     def at(dx, dy):
         return lax.rem(gx + dx + ngx, ngx), lax.rem(gy + dy + ngy, ngy)
 
@@ -175,10 +168,8 @@
         tx, ty = lax.div(tile, ngy), lax.rem(tile, ngy)
         return [ref_s[2 * ty + r % 2, 2 * tx + r // 2] for r in range(4)]
 
-    load_s.wait()
     mine = flags_of(me)
     lane8, lane32, lane40 = lanes(8), lanes(32), lanes(EXT)
-    load.wait()
 
     zero8 = jnp.zeros((8, 128), F32)
     peak = zero8
@@ -296,7 +287,6 @@
     for copy in round2:
         copy.start()
 
-    load_v.wait()
     tile_of = lax.broadcasted_iota(jnp.int32, (2 * ngy, 2 * ngx), 1) // 2 * ngy
     tile_of = tile_of + lax.broadcasted_iota(jnp.int32, (2 * ngy, 2 * ngx), 0) // 2
     before = jnp.sum(jnp.where(tile_of < me, ref_v[...], 0))
@@ -510,9 +500,6 @@
 def shards(ngx, ngy, fields, refined):
     vmem = lambda *shape: pltpu.VMEM(shape, F32)
     scratch = [
-        pltpu.SMEM((2 * ngy, 2 * ngx), jnp.int32),
-        pltpu.VMEM((2 * ngy, 2 * ngx), jnp.int32),
-        vmem(8, 32, 512),
         vmem(8, 2, BS, 128),
         vmem(8, PAD_ROWS, 128),
         vmem(6, 8, EXT, 128),
@@ -535,7 +522,6 @@
         vmem(8, EXT, 128),
         vmem(8, EXT, 128),
         vmem(4, 8, BS, 128),
-        pltpu.SemaphoreType.DMA((3,)),
         pltpu.SemaphoreType.DMA((ngx + ngy + 8,)),
         pltpu.SemaphoreType.DMA((ngx + ngy + 8,)),
     ]
@@ -543,15 +529,16 @@
         functools.partial(kernel, ngx, ngy),
         out_shape=jax.ShapeDtypeStruct((8, BS, CAP * BS), F32),
         in_specs=[
-            pl.BlockSpec(memory_space=pltpu.HBM),
-            pl.BlockSpec(memory_space=pltpu.HBM),
+            pl.BlockSpec(memory_space=pltpu.SMEM),
+            pl.BlockSpec(memory_space=pltpu.VMEM),
+            pl.BlockSpec(memory_space=pltpu.VMEM),
         ],
         out_specs=pl.BlockSpec(memory_space=pltpu.VMEM),
         scratch_shapes=scratch,
         compiler_params=pltpu.CompilerParams(
-            collective_id=0, has_side_effects=True, vmem_limit_bytes=60 * 1024 * 1024
+            collective_id=0, has_side_effects=True, vmem_limit_bytes=32 * 1024 * 1024
         ),
-    )(refined.T, fields)
+    )(refined.T, refined.T, fields)
 
 
 def solution(mesh):

time: 28.3 us -> 29 us (1.025)
  local copies, waits for them, and re-layouts: 1.77 us -> 2.49 us
    unnamed x1 -> x5, local copies, waits for them, and re-layouts: 1.77 us -> 2.49 us
where the time goes in v3:
time: 29 us; the launch traced here: 28.8 us
  Pallas kernels  26.3 us (91%)
  local copies, waits for them, and re-layouts  2.49 us (9%)
    pallas_call x1, Pallas kernels, shards(): pl.pallas_call(functools.partial(kernel, ngx, ngy), out_shape=jax.ShapeDt...  26.3 us
    unnamed x5, local copies, waits for them, and re-layouts  2.49 us

profile of v3, /device:TPU:0, one launch (start us, length us, event | category | flops | bytes accessed | tf_op | source)
XLA Modules:
  0.0 28.8 jit_solution(1509392312342993094)
XLA Ops:
  0.0 0.0 copy-start
  0.0 1.0 %copy-done = f32[8,32,512]{2,1,0:T(8,128)S(1)} copy-done((f32[8,32,512]{2,1,0:T(8,128)S(1)}, f32[8,32,512]{2,1,0:T(8,128)}, u32[]{:S(2)}) %copy-start) | copy-done | bytes 524312
  1.0 0.0 copy-start.1
  1.0 0.7 %copy-done.1 = s32[32,16]{0,1:T(8,128)S(1)} copy-done((s32[32,16]{0,1:T(8,128)S(1)}, s32[32,16]{0,1:T(8,128)}, u32[]{:S(2)}) %copy-start.1) | copy-done | bytes 2072
  1.7 26.3 %shard_map.28 = f32[8,32,320]{2,1,0:T(8,128)S(1)} custom-call(s32[16,32]{1,0:T(8,128)S(1)} %bitcast.1, s32[16,32]{1,0:T(8,128)S(1)} %bitcast.2, f32[8,32,512]{2,1,0:T(8,128)S(1)} %copy-done), custom_call_target="tpu_custom_call" | custom-call | tf_op jit(solution)/shard_map/pallas_call | solution.py:528
  28.1 0.7 %copy.4 = f32[8,32,320]{2,1,0:T(8,128)} copy(f32[8,32,320]{2,1,0:T(8,128)S(1)} %shard_map.28) | data formatting | bytes 655360
Async XLA Ops:
  0.0 1.0 %copy-start = (f32[8,32,512]{2,1,0:T(8,128)S(1)}, f32[8,32,512]{2,1,0:T(8,128)}, u32[]{:S(2)}) copy-start(f32[8,32,512]{2,1,0:T(8,128)} %X.1) | copy-start | bytes 1572868
  1.0 0.7 %copy-start.1 = (s32[32,16]{0,1:T(8,128)S(1)}, s32[32,16]{0,1:T(8,128)}, u32[]{:S(2)}) copy-start(s32[32,16]{0,1:T(8,128)} %param.3) | copy-start | bytes 6148

commit v4 on v2

--- a/solution.py
+++ b/solution.py
@@ -38,8 +38,7 @@
 
 
 def recip(x):
-    r = pltpu.reciprocal(x, approx=True)
-    return r * (2.0 - x * r)
+    return pltpu.reciprocal(x, approx=True)
 
 
 def root(x):
@@ -143,7 +142,7 @@
 
 
 def kernel(ngx, ngy, refined, fields, out, *scratch):
-    (ref_s, ref_v, X, Z, G, U, ML, MR, SR, RB, SK, RK, SY, RY, VM, P1, P2, SX, GX, DY, W, RA, EA, GX2, O, in_sem, send, recv) = scratch
+    (ref_s, ref_v, X, Z, G, U, ML, MR, SR, RB, SK, RK, SY, RY, VM, VS, P1, P2, SX, GX, DY, W, RA, EA, GX2, O, in_sem, send, recv) = scratch
     gx = lax.axis_index("gx")
     gy = lax.axis_index("gy")
     me = gx * ngy + gy
@@ -192,11 +191,7 @@
             fast_x, fast_y = fast_pair(inv, pressure, half_b2, yy + zz, xx + zz)
             rate = jnp.maximum(jnp.abs(vx) + fast_x, jnp.abs(vy) + fast_y)
             peak = jnp.maximum(peak, jnp.where(weight > 0.0, rate * weight, 0.0))
-    VM[0] = peak
-    round1 = [remote(VM.at[0], P1.at[s - 1], at(0, s)) for s in range(1, ngy)]
-    pl.semaphore_wait(barrier, len(partners))
-    for copy in round1:
-        copy.start()
+    VS[0] = jnp.max(peak, axis=0, keepdims=True)
 
     def rotate(h, carry):
         for cc in range(4):
@@ -260,9 +255,6 @@
 
     pack_columns()
 
-    ghosts = [remote(SY.at[0], RY.at[0], at(0, 1)), remote(SY.at[1], RY.at[1], at(0, -1))]
-    for copy in ghosts:
-        copy.start()
     def pack_rows():
         for d in range(2):
             corner = zero8
@@ -275,7 +267,9 @@
 
     pack_rows()
 
-    edges = [
+    ghosts = [
+        remote(SY.at[0], RY.at[0], at(0, 1)),
+        remote(SY.at[1], RY.at[1], at(0, -1)),
         remote(SR.at[0], RB.at[0], at(1, 0)),
         remote(SR.at[1], RB.at[1], at(-1, 0)),
         remote(SK.at[0], RK.at[0], at(1, 1)),
@@ -283,17 +277,9 @@
         remote(SK.at[1], RK.at[2], at(-1, 1)),
         remote(SK.at[1], RK.at[3], at(-1, -1)),
     ]
-    for copy in edges:
-        copy.start()
-    ghosts += edges
-
-    for copy in round1:
-        copy.wait_recv()
-    for s in range(ngy - 1):
-        peak = jnp.maximum(peak, P1[s])
-    VM[1] = peak
-    round2 = [remote(VM.at[1], P2.at[s - 1], at(s, 0)) for s in range(1, ngx)]
-    for copy in round2:
+    round1 = [remote(VS.at[0], P1.at[s - 1], at(0, s)) for s in range(1, ngy)]
+    pl.semaphore_wait(barrier, len(partners))
+    for copy in ghosts + round1:
         copy.start()
 
     load_v.wait()
@@ -337,6 +323,16 @@
         if w >= 7:
             flag = jnp.where(index < count, flag, find(index - count, following)[2])
         wide[w] = 0.5 + 0.5 * flag.astype(F32)
+
+    for copy in round1:
+        copy.wait_recv()
+    top = VS[0]
+    for s in range(ngy - 1):
+        top = jnp.maximum(top, P1[s])
+    VS[1] = top
+    round2 = [remote(VS.at[1], P2.at[s - 1], at(s, 0)) for s in range(1, ngx)]
+    for copy in round2:
+        copy.start()
 
     for copy in ghosts:
         copy.wait_recv()
@@ -420,9 +416,9 @@
     for copy in round2:
         copy.wait_recv()
     for s in range(ngx - 1):
-        peak = jnp.maximum(peak, P2[s])
-    peak = jnp.max(jnp.max(peak, axis=0, keepdims=True), axis=1, keepdims=True)
-    time_step = COURANT / jnp.broadcast_to(peak, (8, 128))
+        top = jnp.maximum(top, P2[s])
+    top = jnp.max(top, axis=1, keepdims=True)
+    time_step = COURANT / jnp.broadcast_to(top, (8, 128))
 
     def widths(ws):
         v = jnp.full((8, 128), wide[ws[0]], F32)
@@ -430,13 +426,13 @@
             v = jnp.where(lane8 < EXT * (g + 1), v, wide[w])
         return v
 
-    VM[2] = time_step * widths((3, 4, 5))
-    VM[3] = time_step * widths((6,))
-    VM[4] = time_step * widths((0, 1, 2))
-    VM[5] = time_step * widths((7, 8, 9))
+    VM[0] = time_step * widths((3, 4, 5))
+    VM[1] = time_step * widths((6,))
+    VM[2] = time_step * widths((0, 1, 2))
+    VM[3] = time_step * widths((7, 8, 9))
 
     def second(t, carry, pick=lambda t: t):
-        rate = VM[2 + t]
+        rate = VM[t]
         at_u = pick(t)
         half = 0.5 * rate
         for r in MID:
@@ -480,6 +476,15 @@
 
     lax.fori_loop(0, 2, second, 0)
 
+    def finish_local():
+        for c in range(8):
+            o0, o1 = O[0, c], O[1, c]
+            out[c, :, 0:128] = roll(o0, 92)
+            x = jnp.where(lane32 < 64, roll(o0, -52), roll(o1, 60))
+            out[c, :, 128:256] = jnp.where(lane32 < 32, roll(o0, -44), x)
+
+    finish_local()
+
     for copy in moves:
         copy.wait_recv()
 
@@ -493,13 +498,12 @@
 
     def finish():
         for c in range(8):
-            o = [O[t, c] for t in range(4)]
-            o0 = jnp.where(lane32 < 32, roll(o[2], -4), jnp.where(lane32 < 64, roll(o[2], -12), roll(o[2], -20)))
-            out[c, :, 0:128] = jnp.where(lane32 < 96, o0, roll(o[0], 92))
-            o1 = jnp.where(lane32 < 32, roll(o[0], -44), roll(o[0], -52))
-            out[c, :, 128:256] = jnp.where(lane32 < 64, o1, jnp.where(lane32 < 96, roll(o[1], 60), roll(o[3], 92)))
-            o2 = jnp.where(lane32 < 32, roll(o[3], -44), roll(o[3], -52))
-            out[c, :, 256:320] = o2[:, 0:64]
+            o2, o3 = O[2, c], O[3, c]
+            x = jnp.where(lane32 < 32, roll(o2, -4), jnp.where(lane32 < 64, roll(o2, -12), roll(o2, -20)))
+            pltpu.store(out.at[c, :, pl.ds(0, 128)], x, mask=lane32 < 96)
+            pltpu.store(out.at[c, :, pl.ds(128, 128)], roll(o3, 92), mask=lane32 >= 96)
+            x = jnp.where(lane32 < 32, roll(o3, -44), roll(o3, -52))
+            out[c, :, 256:320] = x[:, 0:64]
 
     finish()
 
@@ -524,9 +528,10 @@
         vmem(4, 8, 128),
         vmem(2, 2, 32, 128),
         vmem(2, 2, 32, 128),
-        vmem(6, 8, 128),
-        vmem(ngy - 1, 8, 128),
-        vmem(ngx - 1, 8, 128),
+        vmem(4, 8, 128),
+        vmem(2, 1, 128),
+        vmem(ngy - 1, 1, 128),
+        vmem(ngx - 1, 1, 128),
         vmem(8, EXT, 128),
         vmem(4, 8, EXT, 128),
         vmem(4, 8, EXT, 128),
@@ -549,7 +554,7 @@
         out_specs=pl.BlockSpec(memory_space=pltpu.VMEM),
         scratch_shapes=scratch,
         compiler_params=pltpu.CompilerParams(
-            collective_id=0, has_side_effects=True, vmem_limit_bytes=60 * 1024 * 1024
+            collective_id=0, has_side_effects=True, vmem_limit_bytes=56_000_000
         ),
     )(refined.T, fields)
 

time: 28.3 us -> 25.5 us (0.901)
  Pallas kernels: 26.4 us -> 23.8 us
  local copies, waits for them, and re-layouts: 1.77 us -> 1.44 us
    pallas_call x1, Pallas kernels: 26.4 us -> 23.8 us  [shards(): pl.pallas_call(functools.partial(kernel, ngx, ngy), out_shape=jax.ShapeDt...]
    unnamed x1 -> x3, local copies, waits for them, and re-layouts: 1.77 us -> 1.44 us
where the time goes in v4:
time: 25.5 us; the launch traced here: 25.3 us
  Pallas kernels  23.8 us (93%)
  local copies, waits for them, and re-layouts  1.44 us (6%)
    pallas_call x1, Pallas kernels, shards(): pl.pallas_call(functools.partial(kernel, ngx, ngy), out_shape=jax.ShapeDt...  23.8 us
    unnamed x3, local copies, waits for them, and re-layouts  1.44 us

profile of v4, /device:TPU:0, one launch (start us, length us, event | category | flops | bytes accessed | tf_op | source)
XLA Modules:
  0.0 25.3 jit_solution(7467153348770811122)
XLA Ops:
  0.0 0.0 copy-start
  0.0 0.7 %copy-done = s32[32,16]{0,1:T(8,128)S(1)} copy-done((s32[32,16]{0,1:T(8,128)S(1)}, s32[32,16]{0,1:T(8,128)}, u32[]{:S(2)}) %copy-start) | copy-done | bytes 2072
  0.7 23.8 %shard_map.28 = f32[8,32,320]{2,1,0:T(8,128)S(1)} custom-call(s32[16,32]{1,0:T(8,128)S(1)} %bitcast.1, f32[8,32,512]{2,1,0:T(8,128)} %fields.1), custom_call_target="tpu_custom_call" | custom-call | tf_op jit(solution)/shard_map/pallas_call | solution.py:547
  24.5 0.7 %copy.4 = f32[8,32,320]{2,1,0:T(8,128)} copy(f32[8,32,320]{2,1,0:T(8,128)S(1)} %shard_map.28) | data formatting | bytes 655360
Async XLA Ops:
  0.0 0.7 %copy-start = (s32[32,16]{0,1:T(8,128)S(1)}, s32[32,16]{0,1:T(8,128)}, u32[]{:S(2)}) copy-start(s32[32,16]{0,1:T(8,128)} %param.3) | copy-start | bytes 6148

commit v5 on v4

--- a/solution.py
+++ b/solution.py
@@ -279,7 +279,7 @@
     ]
     round1 = [remote(VS.at[0], P1.at[s - 1], at(0, s)) for s in range(1, ngy)]
     pl.semaphore_wait(barrier, len(partners))
-    for copy in ghosts + round1:
+    for copy in ghosts[2:] + ghosts[:2] + round1:
         copy.start()
 
     load_v.wait()
@@ -324,6 +324,24 @@
             flag = jnp.where(index < count, flag, find(index - count, following)[2])
         wide[w] = 0.5 + 0.5 * flag.astype(F32)
 
+    left8, right8 = lane8 >= 124, lane8 < 4
+    left32, right32 = lane32 >= 124, lane32 < 4
+
+    def fill_lanes():
+        for h in range(2):
+            low4 = lane32 % 8 < 4
+            pair = (jnp.where(low4, RY[0, h], RY[1, h]), jnp.where(low4, RY[1, h], RY[0, h]))
+            for cc in range(4):
+                for k in range(6):
+                    x = roll(pair[k % 2], -(32 * cc + 4 * k) - 4)
+                    for i, mask in enumerate((left32, right32)):
+                        row = FINE[i] + 4 + 32 * k if k < 4 else COARSE[i] + 4 + 32 * (k - 4)
+                        pltpu.store(G.at[4 * h + cc, pl.ds(row, 32), :], x, mask=mask)
+
+    for copy in ghosts[:2]:
+        copy.wait_recv()
+    fill_lanes()
+
     for copy in round1:
         copy.wait_recv()
     top = VS[0]
@@ -334,11 +352,7 @@
     for copy in round2:
         copy.start()
 
-    for copy in ghosts:
-        copy.wait_recv()
-    def fill():
-        left8, right8 = lane8 >= 124, lane8 < 4
-        left32, right32 = lane32 >= 124, lane32 < 4
+    def fill_rows():
         for d in range(2):
             corner = jnp.where(lane8 % 8 < 4, RK[2 * d], RK[2 * d + 1])
             for c in range(8):
@@ -349,35 +363,32 @@
                     fine, coarse = FINE[i] + 132 * d, COARSE[i] + 68 * d
                     G[c, fine : fine + 4, :] = x[0:4]
                     G[c, coarse : coarse + 4, :] = x[4:8]
-        for h in range(2):
-            low4 = lane32 % 8 < 4
-            pair = (jnp.where(low4, RY[0, h], RY[1, h]), jnp.where(low4, RY[1, h], RY[0, h]))
-            for cc in range(4):
-                for k in range(6):
-                    x = roll(pair[k % 2], -(32 * cc + 4 * k) - 4)
-                    for i, mask in enumerate((left32, right32)):
-                        row = FINE[i] + 4 + 32 * k if k < 4 else COARSE[i] + 4 + 32 * (k - 4)
-                        pltpu.store(G.at[4 * h + cc, pl.ds(row, 32), :], x, mask=mask)
-
-    fill()
-
-    def gather(dst, which):
-        for c in range(8):
+
+    for copy in ghosts[2:]:
+        copy.wait_recv()
+    fill_rows()
+
+    def gather(dst, which, some=range(8)):
+        for c in some:
             parts = [roll(G[c, pl.ds(place[w][0], EXT), :], EXT * g - place[w][1]) for g, w in enumerate(which)]
             x = parts[0]
             for g, part in enumerate(parts[1:]):
                 x = jnp.where(lane40 < EXT * (g + 1), x, part)
             dst[c] = x
 
-    gather(MR, (10, 11, 12))
-    gather(ML, (-3, -2, -1))
     carry_up = lax.div(gy + 1, ngy)
     carry_down = lax.div(ngy - gy, ngy)
     ahead = (lax.rem(gx + carry_up, ngx), lax.rem(gy + 1, ngy))
     behind = (lax.rem(gx + ngx - carry_down, ngx), lax.rem(gy + ngy - 1, ngy))
-    moves = [remote(MR, U.at[4], ahead), remote(ML, U.at[5], behind)]
-    for copy in moves:
-        copy.start()
+    moves = []
+    for part in range(2):
+        gather(MR, (10, 11, 12), range(4 * part, 4 * part + 4))
+        gather(ML, (-3, -2, -1), range(4 * part, 4 * part + 4))
+        some = pl.ds(4 * part, 4)
+        moves.append(remote(MR.at[some], U.at[4, some], ahead))
+        moves.append(remote(ML.at[some], U.at[5, some], behind))
+        for copy in moves[-2:]:
+            copy.start()
 
     gather(U.at[0], (3, 4, 5))
     gather(U.at[1], (6,))
@@ -541,8 +552,8 @@
         vmem(8, EXT, 128),
         vmem(4, 8, BS, 128),
         pltpu.SemaphoreType.DMA((3,)),
-        pltpu.SemaphoreType.DMA((ngx + ngy + 8,)),
-        pltpu.SemaphoreType.DMA((ngx + ngy + 8,)),
+        pltpu.SemaphoreType.DMA((ngx + ngy + 10,)),
+        pltpu.SemaphoreType.DMA((ngx + ngy + 10,)),
     ]
     return pl.pallas_call(
         functools.partial(kernel, ngx, ngy),

time: 25.5 us -> 25.2 us (0.988)
  Pallas kernels: 23.8 us -> 23.5 us
    pallas_call x1, Pallas kernels: 23.8 us -> 23.5 us  [shards(): pl.pallas_call(functools.partial(kernel, ngx, ngy), out_shape=jax.ShapeDt...]
where the time goes in v5:
time: 25.2 us; the launch traced here: 25 us
  Pallas kernels  23.5 us (93%)
  local copies, waits for them, and re-layouts  1.44 us (6%)
    pallas_call x1, Pallas kernels, shards(): pl.pallas_call(functools.partial(kernel, ngx, ngy), out_shape=jax.ShapeDt...  23.5 us
    unnamed x3, local copies, waits for them, and re-layouts  1.44 us

profile of v5, /device:TPU:0, one launch (start us, length us, event | category | flops | bytes accessed | tf_op | source)
XLA Modules:
  0.0 25.0 jit_solution(8757411678482848077)
XLA Ops:
  0.0 0.0 copy-start
  0.0 0.7 %copy-done = s32[32,16]{0,1:T(8,128)S(1)} copy-done((s32[32,16]{0,1:T(8,128)S(1)}, s32[32,16]{0,1:T(8,128)}, u32[]{:S(2)}) %copy-start) | copy-done | bytes 2072
  0.7 23.5 %shard_map.28 = f32[8,32,320]{2,1,0:T(8,128)S(1)} custom-call(s32[16,32]{1,0:T(8,128)S(1)} %bitcast.1, f32[8,32,512]{2,1,0:T(8,128)} %fields.1), custom_call_target="tpu_custom_call" | custom-call | tf_op jit(solution)/shard_map/pallas_call | solution.py:558
  24.2 0.7 %copy.4 = f32[8,32,320]{2,1,0:T(8,128)} copy(f32[8,32,320]{2,1,0:T(8,128)S(1)} %shard_map.28) | data formatting | bytes 655360
Async XLA Ops:
  0.0 0.7 %copy-start = (s32[32,16]{0,1:T(8,128)S(1)}, s32[32,16]{0,1:T(8,128)}, u32[]{:S(2)}) copy-start(s32[32,16]{0,1:T(8,128)} %param.3) | copy-start | bytes 6148

commit v6 on v5

--- a/solution.py
+++ b/solution.py
@@ -43,6 +43,16 @@
 
 def root(x):
     return x * lax.rsqrt(jnp.maximum(x, 1e-30))
+
+
+def farthest(count, minor):
+    major = max(count // minor, 1)
+
+    def hops(step):
+        outer, inner = step // minor, step % minor
+        return min(outer, major - outer) + min(inner, minor - inner)
+
+    return sorted(range(1, count), key=lambda step: -hops(step))
 
 
 def limited(value, other):
@@ -277,7 +287,7 @@
         remote(SK.at[1], RK.at[2], at(-1, 1)),
         remote(SK.at[1], RK.at[3], at(-1, -1)),
     ]
-    round1 = [remote(VS.at[0], P1.at[s - 1], at(0, s)) for s in range(1, ngy)]
+    round1 = [remote(VS.at[0], P1.at[s - 1], at(0, s)) for s in farthest(ngy, 2)]
     pl.semaphore_wait(barrier, len(partners))
     for copy in ghosts[2:] + ghosts[:2] + round1:
         copy.start()
@@ -348,7 +358,7 @@
     for s in range(ngy - 1):
         top = jnp.maximum(top, P1[s])
     VS[1] = top
-    round2 = [remote(VS.at[1], P2.at[s - 1], at(s, 0)) for s in range(1, ngx)]
+    round2 = [remote(VS.at[1], P2.at[s - 1], at(s, 0)) for s in farthest(ngx, 4)]
     for copy in round2:
         copy.start()
 
@@ -424,6 +434,19 @@
 
     lax.fori_loop(0, 2, first, 0)
 
+    def widths(ws):
+        v = jnp.full((8, 128), wide[ws[0]], F32)
+        for g, w in enumerate(ws[1:]):
+            v = jnp.where(lane8 < EXT * (g + 1), v, wide[w])
+        return v
+
+    VM[0] = widths((3, 4, 5))
+    VM[1] = widths((6,))
+    VM[2] = widths((0, 1, 2))
+    VM[3] = widths((7, 8, 9))
+
+    for copy in ghosts + round1 + moves + round2:
+        copy.wait_send()
     for copy in round2:
         copy.wait_recv()
     for s in range(ngx - 1):
@@ -431,19 +454,8 @@
     top = jnp.max(top, axis=1, keepdims=True)
     time_step = COURANT / jnp.broadcast_to(top, (8, 128))
 
-    def widths(ws):
-        v = jnp.full((8, 128), wide[ws[0]], F32)
-        for g, w in enumerate(ws[1:]):
-            v = jnp.where(lane8 < EXT * (g + 1), v, wide[w])
-        return v
-
-    VM[0] = time_step * widths((3, 4, 5))
-    VM[1] = time_step * widths((6,))
-    VM[2] = time_step * widths((0, 1, 2))
-    VM[3] = time_step * widths((7, 8, 9))
-
     def second(t, carry, pick=lambda t: t):
-        rate = VM[t]
+        rate = time_step * VM[t]
         at_u = pick(t)
         half = 0.5 * rate
         for r in MID:
@@ -517,9 +529,6 @@
             out[c, :, 256:320] = x[:, 0:64]
 
     finish()
-
-    for copy in ghosts + moves + round1 + round2:
-        copy.wait_send()
 
 
 def shards(ngx, ngy, fields, refined):

time: 25.2 us -> 25.1 us (level)
  no operation moved by 1% of the time
where the time goes in v6:
time: 25.1 us; the launch traced here: 24.9 us
  Pallas kernels  23.5 us (94%)
  local copies, waits for them, and re-layouts  1.44 us (6%)
    pallas_call x1, Pallas kernels, shards(): pl.pallas_call(functools.partial(kernel, ngx, ngy), out_shape=jax.ShapeDt...  23.5 us
    unnamed x3, local copies, waits for them, and re-layouts  1.44 us

profile of v6, /device:TPU:0, one launch (start us, length us, event | category | flops | bytes accessed | tf_op | source)
XLA Modules:
  0.0 24.9 jit_solution(12741419076449155221)
XLA Ops:
  0.0 0.0 copy-start
  0.0 0.7 %copy-done = s32[32,16]{0,1:T(8,128)S(1)} copy-done((s32[32,16]{0,1:T(8,128)S(1)}, s32[32,16]{0,1:T(8,128)}, u32[]{:S(2)}) %copy-start) | copy-done | bytes 2072
  0.7 23.5 %shard_map.28 = f32[8,32,320]{2,1,0:T(8,128)S(1)} custom-call(s32[16,32]{1,0:T(8,128)S(1)} %bitcast.1, f32[8,32,512]{2,1,0:T(8,128)} %fields.1), custom_call_target="tpu_custom_call" | custom-call | tf_op jit(solution)/shard_map/pallas_call | solution.py:567
  24.2 0.7 %copy.4 = f32[8,32,320]{2,1,0:T(8,128)} copy(f32[8,32,320]{2,1,0:T(8,128)S(1)} %shard_map.28) | data formatting | bytes 655360
Async XLA Ops:
  0.0 0.7 %copy-start = (s32[32,16]{0,1:T(8,128)S(1)}, s32[32,16]{0,1:T(8,128)}, u32[]{:S(2)}) copy-start(s32[32,16]{0,1:T(8,128)} %param.3) | copy-start | bytes 6148

commit v7 on v6

--- a/solution.py
+++ b/solution.py
@@ -434,6 +434,16 @@
 
     lax.fori_loop(0, 2, first, 0)
 
+    for copy in moves:
+        copy.wait_recv()
+
+    def pick(t):
+        from_left = jnp.where(excess > 0, 4, 2)
+        from_right = jnp.where(excess + count < CAP, 5, 3)
+        return jnp.where(t == 2, from_left, jnp.where(t == 3, from_right, t))
+
+    lax.fori_loop(2, 4, functools.partial(first, pick=pick), 0)
+
     def widths(ws):
         v = jnp.full((8, 128), wide[ws[0]], F32)
         for g, w in enumerate(ws[1:]):
@@ -454,7 +464,7 @@
     top = jnp.max(top, axis=1, keepdims=True)
     time_step = COURANT / jnp.broadcast_to(top, (8, 128))
 
-    def second(t, carry, pick=lambda t: t):
+    def second(t, carry):
         rate = time_step * VM[t]
         at_u = pick(t)
         half = 0.5 * rate
@@ -497,7 +507,7 @@
                 O[t, c, r - 4 : r + 4, :] = U[at_u, c, r : r + 8, :] - rate * change
         return carry
 
-    lax.fori_loop(0, 2, second, 0)
+    lax.fori_loop(0, 4, second, 0)
 
     def finish_local():
         for c in range(8):
@@ -508,16 +518,6 @@
 
     finish_local()
 
-    for copy in moves:
-        copy.wait_recv()
-
-    def pick(t):
-        from_left = jnp.where(excess > 0, 4, 2)
-        from_right = jnp.where(excess + count < CAP, 5, 3)
-        return jnp.where(t == 2, from_left, jnp.where(t == 3, from_right, t))
-
-    lax.fori_loop(2, 4, functools.partial(first, pick=pick), 0)
-    lax.fori_loop(2, 4, functools.partial(second, pick=pick), 0)
 
     def finish():
         for c in range(8):

time: 25.1 us -> 26.9 us (1.072)
  Pallas kernels: 23.5 us -> 25.2 us
    pallas_call x1, Pallas kernels: 23.5 us -> 25.2 us  [shards(): pl.pallas_call(functools.partial(kernel, ngx, ngy), out_shape=jax.ShapeDt...]
where the time goes in v7:
time: 26.9 us; the launch traced here: 26.7 us
  Pallas kernels  25.2 us (94%)
  local copies, waits for them, and re-layouts  1.44 us (5%)
    pallas_call x1, Pallas kernels, shards(): pl.pallas_call(functools.partial(kernel, ngx, ngy), out_shape=jax.ShapeDt...  25.2 us
    unnamed x3, local copies, waits for them, and re-layouts  1.44 us

profile of v7, /device:TPU:0, one launch (start us, length us, event | category | flops | bytes accessed | tf_op | source)
XLA Modules:
  0.0 26.7 jit_solution(17121463253165210836)
XLA Ops:
  0.0 0.0 copy-start
  0.0 0.7 %copy-done = s32[32,16]{0,1:T(8,128)S(1)} copy-done((s32[32,16]{0,1:T(8,128)S(1)}, s32[32,16]{0,1:T(8,128)}, u32[]{:S(2)}) %copy-start) | copy-done | bytes 2072
  0.7 25.2 %shard_map.28 = f32[8,32,320]{2,1,0:T(8,128)S(1)} custom-call(s32[16,32]{1,0:T(8,128)S(1)} %bitcast.1, f32[8,32,512]{2,1,0:T(8,128)} %fields.1), custom_call_target="tpu_custom_call" | custom-call | tf_op jit(solution)/shard_map/pallas_call | solution.py:567
  26.0 0.7 %copy.4 = f32[8,32,320]{2,1,0:T(8,128)} copy(f32[8,32,320]{2,1,0:T(8,128)S(1)} %shard_map.28) | data formatting | bytes 655360
Async XLA Ops:
  0.0 0.7 %copy-start = (s32[32,16]{0,1:T(8,128)S(1)}, s32[32,16]{0,1:T(8,128)}, u32[]{:S(2)}) copy-start(s32[32,16]{0,1:T(8,128)} %param.3) | copy-start | bytes 6148

commit v8 on v6

--- a/solution.py
+++ b/solution.py
@@ -352,16 +352,6 @@
         copy.wait_recv()
     fill_lanes()
 
-    for copy in round1:
-        copy.wait_recv()
-    top = VS[0]
-    for s in range(ngy - 1):
-        top = jnp.maximum(top, P1[s])
-    VS[1] = top
-    round2 = [remote(VS.at[1], P2.at[s - 1], at(s, 0)) for s in farthest(ngx, 4)]
-    for copy in round2:
-        copy.start()
-
     def fill_rows():
         for d in range(2):
             corner = jnp.where(lane8 % 8 < 4, RK[2 * d], RK[2 * d + 1])
@@ -399,6 +389,16 @@
         moves.append(remote(ML.at[some], U.at[5, some], behind))
         for copy in moves[-2:]:
             copy.start()
+
+    for copy in round1:
+        copy.wait_recv()
+    top = VS[0]
+    for s in range(ngy - 1):
+        top = jnp.maximum(top, P1[s])
+    VS[1] = top
+    round2 = [remote(VS.at[1], P2.at[s - 1], at(s, 0)) for s in farthest(ngx, 4)]
+    for copy in round2:
+        copy.start()
 
     gather(U.at[0], (3, 4, 5))
     gather(U.at[1], (6,))

time: 25.1 us -> 25.2 us (level)
  no operation moved by 1% of the time
where the time goes in v8:
time: 25.2 us; the launch traced here: 25 us
  Pallas kernels  23.5 us (93%)
  local copies, waits for them, and re-layouts  1.44 us (6%)
    pallas_call x1, Pallas kernels, shards(): pl.pallas_call(functools.partial(kernel, ngx, ngy), out_shape=jax.ShapeDt...  23.5 us
    unnamed x3, local copies, waits for them, and re-layouts  1.44 us

profile of v8, /device:TPU:0, one launch (start us, length us, event | category | flops | bytes accessed | tf_op | source)
XLA Modules:
  0.0 25.0 jit_solution(11478862655356284173)
XLA Ops:
  0.0 0.0 copy-start
  0.0 0.7 %copy-done = s32[32,16]{0,1:T(8,128)S(1)} copy-done((s32[32,16]{0,1:T(8,128)S(1)}, s32[32,16]{0,1:T(8,128)}, u32[]{:S(2)}) %copy-start) | copy-done | bytes 2072
  0.7 23.5 %shard_map.28 = f32[8,32,320]{2,1,0:T(8,128)S(1)} custom-call(s32[16,32]{1,0:T(8,128)S(1)} %bitcast.1, f32[8,32,512]{2,1,0:T(8,128)} %fields.1), custom_call_target="tpu_custom_call" | custom-call | tf_op jit(solution)/shard_map/pallas_call | solution.py:567
  24.2 0.7 %copy.4 = f32[8,32,320]{2,1,0:T(8,128)} copy(f32[8,32,320]{2,1,0:T(8,128)S(1)} %shard_map.28) | data formatting | bytes 655360
Async XLA Ops:
  0.0 0.7 %copy-start = (s32[32,16]{0,1:T(8,128)S(1)}, s32[32,16]{0,1:T(8,128)}, u32[]{:S(2)}) copy-start(s32[32,16]{0,1:T(8,128)} %param.3) | copy-start | bytes 6148

commit v9 on v8

--- a/solution.py
+++ b/solution.py
@@ -381,7 +381,8 @@
     ahead = (lax.rem(gx + carry_up, ngx), lax.rem(gy + 1, ngy))
     behind = (lax.rem(gx + ngx - carry_down, ngx), lax.rem(gy + ngy - 1, ngy))
     moves = []
-    for part in range(2):
+
+    def migrate(part):
         gather(MR, (10, 11, 12), range(4 * part, 4 * part + 4))
         gather(ML, (-3, -2, -1), range(4 * part, 4 * part + 4))
         some = pl.ds(4 * part, 4)
@@ -390,6 +391,7 @@
         for copy in moves[-2:]:
             copy.start()
 
+    migrate(0)
     for copy in round1:
         copy.wait_recv()
     top = VS[0]
@@ -399,6 +401,7 @@
     round2 = [remote(VS.at[1], P2.at[s - 1], at(s, 0)) for s in farthest(ngx, 4)]
     for copy in round2:
         copy.start()
+    migrate(1)
 
     gather(U.at[0], (3, 4, 5))
     gather(U.at[1], (6,))

time: 25.2 us -> 25.2 us (level)
  no operation moved by 1% of the time
where the time goes in v9:
time: 25.2 us; the launch traced here: 25 us
  Pallas kernels  23.5 us (93%)
  local copies, waits for them, and re-layouts  1.44 us (6%)
    pallas_call x1, Pallas kernels, shards(): pl.pallas_call(functools.partial(kernel, ngx, ngy), out_shape=jax.ShapeDt...  23.5 us
    unnamed x3, local copies, waits for them, and re-layouts  1.44 us

profile of v9, /device:TPU:0, one launch (start us, length us, event | category | flops | bytes accessed | tf_op | source)
XLA Modules:
  0.0 25.0 jit_solution(2943806716217551774)
XLA Ops:
  0.0 0.0 copy-start
  0.0 0.7 %copy-done = s32[32,16]{0,1:T(8,128)S(1)} copy-done((s32[32,16]{0,1:T(8,128)S(1)}, s32[32,16]{0,1:T(8,128)}, u32[]{:S(2)}) %copy-start) | copy-done | bytes 2072
  0.7 23.5 %shard_map.28 = f32[8,32,320]{2,1,0:T(8,128)S(1)} custom-call(s32[16,32]{1,0:T(8,128)S(1)} %bitcast.1, f32[8,32,512]{2,1,0:T(8,128)} %fields.1), custom_call_target="tpu_custom_call" | custom-call | tf_op jit(solution)/shard_map/pallas_call | solution.py:570
  24.2 0.7 %copy.4 = f32[8,32,320]{2,1,0:T(8,128)} copy(f32[8,32,320]{2,1,0:T(8,128)S(1)} %shard_map.28) | data formatting | bytes 655360
Async XLA Ops:
  0.0 0.7 %copy-start = (s32[32,16]{0,1:T(8,128)S(1)}, s32[32,16]{0,1:T(8,128)}, u32[]{:S(2)}) copy-start(s32[32,16]{0,1:T(8,128)} %param.3) | copy-start | bytes 6148
